TPU v7x, 128 devices: a whole 4x4x4 slice. The times are simulated.
128 devices in a mesh: row: 8 (over y_lo, x), col: 16 (over z, y_hi, core).
Axes of the slice: x: 4, y: 4 (y_hi: 2, y_lo: 2; y = y_hi * 2 + y_lo), z: 4, core: 2. Of those that a mesh axis runs over, the one named last changes fastest.
Arguments:
- tokens: bfloat16 [2048, 28672], P('row', 'col'), may hold values from -6 to 6
- edit_src: int32 [512, 4], replicated, may hold values from 0 to 2047
- cov_tiles: float32 [8, 16, 1792, 1792], P('row', 'col'), as said below
- cov_far: float32 [16, 896, 1792], P('col', 'row'), may hold values from -0.03125 to 0.03125
- residual: bfloat16 [8192, 512], P('row'), may hold values from -0.25 to 0.25
Outputs:
- delta: bfloat16 [8192, 28672], P('row', 'col')
Inputs may be any that keep to these rules, and one draw needn't show every extreme that they name: cov_tiles[0, b] is symmetric for every b.
All inputs are finite; a program needn't handle non-finite values.
Results may differ from a plain program's by a relative error of at most 0.024.
Values may be sent and summed in bfloat16 or wider, within the bound.
A program may use at most 128 MiB of HBM per device.

v0:
```python
import jax
import jax.numpy as jnp
from jax import lax
from jax.sharding import PartitionSpec as P


def passed_along(value, axis, steps):
    count = lax.axis_size(axis)
    pairs = [(source, (source + steps) % count) for source in range(count)]
    return lax.ppermute(value, axis, pairs)


def from_partner(value, axis, apart):
    mask = 2**apart
    pairs = [(source, source ^ mask) for source in range(lax.axis_size(axis))]
    return lax.ppermute(value, axis, pairs)


def shards(tokens, edit_src, cov_tiles, cov_far, residual):
    highest = lax.Precision.HIGHEST
    rows_axis = lax.axis_size("row")
    row_at = lax.axis_index("row")
    col_at = lax.axis_index("col")
    tok_dev = tokens.shape[0]
    tile_width = tokens.shape[1]
    relative = edit_src - row_at * tok_dev
    slot_ids = lax.broadcasted_iota(jnp.int32, (1, 1, tok_dev), 2)
    counts = (
        jnp.sum((relative[:, :, None] == slot_ids).astype(jnp.float32), axis=1) / edit_src.shape[1]
    )
    partial_keys = jnp.dot(counts.astype(jnp.bfloat16), tokens, preferred_element_type=jnp.float32)
    own_keys = lax.psum(partial_keys.astype(jnp.bfloat16), "row")
    bit_count = rows_axis.bit_length() - 1
    lagged = own_keys
    for bit_level in range(bit_count):
        shifted = passed_along(lagged, "col", 2**bit_level)
        lagged = jnp.where((row_at >> bit_level) % 2 == 1, shifted, lagged)
    cov_block = cov_tiles[0, 0]
    own_float = own_keys.astype(jnp.float32)
    direct = jnp.dot(
        lagged.astype(jnp.float32), cov_block, precision=highest, preferred_element_type=jnp.float32
    )
    mirror = lax.cond(
        row_at > 0,
        lambda: jnp.dot(
            own_float, cov_block.T, precision=highest, preferred_element_type=jnp.float32
        ),
        lambda: jnp.zeros_like(direct),
    )
    for bit_level in range(bit_count):
        shifted = passed_along(mirror.astype(jnp.bfloat16), "col", -(2**bit_level)).astype(
            mirror.dtype
        )
        mirror = jnp.where((row_at >> bit_level) % 2 == 1, shifted, mirror)
    far_slab = cov_far[0]
    far_rows = far_slab.shape[0]
    low_half = col_at < rows_axis
    half_index = col_at // rows_axis
    offset = half_index * (tile_width // 2) + row_at * far_rows
    other_keys = from_partner(own_keys, "col", bit_count)
    keys_low = jnp.where(low_half, own_keys, other_keys).astype(jnp.float32)
    keys_high = jnp.where(low_half, other_keys, own_keys).astype(jnp.float32)
    picked = lax.dynamic_slice_in_dim(keys_low, offset, far_rows, 1)
    high_term = jnp.dot(picked, far_slab, precision=highest, preferred_element_type=jnp.float32)
    narrow = jnp.dot(keys_high, far_slab.T, precision=highest, preferred_element_type=jnp.float32)
    low_term = lax.dynamic_update_slice_in_dim(jnp.zeros_like(direct), narrow, offset, 1)
    kept_term = jnp.where(low_half, low_term, high_term)
    sent_term = jnp.where(low_half, high_term, low_term)
    far_total = kept_term + from_partner(sent_term.astype(jnp.bfloat16), "col", bit_count).astype(
        sent_term.dtype
    )
    summed = direct + mirror + far_total
    q_block = lax.psum(summed.astype(jnp.bfloat16), "row")
    return jnp.dot(residual, q_block, preferred_element_type=jnp.float32).astype(jnp.bfloat16)


def solution(mesh):
    placed = (
        P("row", "col"),
        P(),
        P("row", "col", None, None),
        P("col", "row", None),
        P("row", None),
    )
    return jax.shard_map(
        shards, mesh=mesh, in_specs=placed, out_specs=P("row", "col"), check_vma=False
    )
```

profile of v0, /device:TPU:0, one launch (start us, length us, event | category | flops | bytes accessed | tf_op | source)
XLA Modules:
  0.0 415.6 jit_solution(1574876981922074789)
XLA Ops:
  7.7 3.1 convolution_convert_fusion.1
  10.8 83.3 %all-reduce.3.cloned.1.call-done = bf16[512,1792]{1,0:T(8,128)(2,1)} async-done(((bf16[512,1792]{1,0:T(8,128)(2,1)}), bf16[512,1792]{1,0:T(8,128)(2,1)}) %all-reduce.3.cloned.1.call-update) | async-done | bytes 1835024 | tf_op jit(solution)/shard_map/psum | solution.py:32
  94.1 2.1 conditional.1
  94.1 2.1 broadcast.10
  96.2 3.4 convert_element_type.56
  99.7 5.4 %collective-permute-start.3 = (bf16[512,1792]{1,0:T(8,128)(2,1)}, bf16[512,1792]{1,0:T(8,128)(2,1)S(1)}, u32[]{:S(2)}, u32[]{:S(2)}) collective-permute-start(bf16[512,1792]{1,0:T(8,128)(2,1)} %convert_element_type.56), channel_id=1, source_target_pairs={{0,15},{1,0},{2,1},{3,2},{4,3},{5,4},{6,5},{7,6},{8,7},{9,8},{10,9... | collective-permute-start | bytes 5505032 | tf_op jit(solution)/shard_map/ppermute | solution.py:10
  105.0 1.9 collective-permute-start.6
  107.0 24.4 %collective-permute-done = bf16[512,1792]{1,0:T(8,128)(2,1)} collective-permute-done((bf16[512,1792]{1,0:T(8,128)(2,1)}, bf16[512,1792]{1,0:T(8,128)(2,1)}, u32[]{:S(2)}, u32[]{:S(2)}) %collective-permute-start) | collective-permute-done | bytes 1835040 | tf_op jit(solution)/shard_map/ppermute | solution.py:10
  131.4 3.0 broadcast_select_fusion
  135.1 6.4 %collective-permute-done.3 = bf16[512,1792]{1,0:T(8,128)(2,1)S(1)} collective-permute-done((bf16[512,1792]{1,0:T(8,128)(2,1)}, bf16[512,1792]{1,0:T(8,128)(2,1)S(1)}, u32[]{:S(2)}, u32[]{:S(2)}) %collective-permute-start.3) | collective-permute-done | bytes 1835040 | tf_op jit(solution)/shard_map/ppermute | solution.py:10
  141.4 1.9 fusion.1
  144.4 56.9 %collective-permute-done.6 = bf16[512,1792]{1,0:T(8,128)(2,1)} collective-permute-done((bf16[512,1792]{1,0:T(8,128)(2,1)}, bf16[512,1792]{1,0:T(8,128)(2,1)}, u32[]{:S(2)}, u32[]{:S(2)}) %collective-permute-start.6) | collective-permute-done | bytes 1835040 | tf_op jit(solution)/shard_map/ppermute | solution.py:16
  201.3 3.3 fusion.2
  204.6 2.1 broadcast.12
  208.5 3.1 broadcast_select_fusion.1
  211.7 5.4 %select_convert_fusion = (bf16[512,1792]{1,0:T(8,128)(2,1)}, f32[512,1792]{1,0:T(8,128)}) fusion(f32[512,1792]{1,0:T(8,128)S(1)} %copy-done.4, pred[]{:T(512)S(6)} %lt.30, f32[1,112,1792]{2,1,0:T(8,128)S(1)} %copy-done.6, bf16[512,1792]{1,0:T(8,128)(2,1)} %collective-permute-done.6, s32[]{:T(128)S(6)} %select_n.96, ...), kind=kOutput, calls=%fused_computation.2 | convolution fusion | flops 1234100224 | bytes 10241536 | tf_op jit(solution)/shard_map/dot_general | solution.py:64
  217.9 3.5 fusion.8
  221.4 2.4 collective-permute-start.5
  223.8 70.5 %collective-permute-done.2 = bf16[512,1792]{1,0:T(8,128)(2,1)} collective-permute-done((bf16[512,1792]{1,0:T(8,128)(2,1)}, bf16[512,1792]{1,0:T(8,128)(2,1)}, u32[]{:S(2)}, u32[]{:S(2)}) %collective-permute-start.2) | collective-permute-done | bytes 1835040 | tf_op jit(solution)/shard_map/ppermute | solution.py:10
  294.3 19.6 %fusion.4 = f32[512,1792]{1,0:T(8,128)} fusion(bf16[512,1792]{1,0:T(8,128)(2,1)} %collective-permute-done.2, bf16[512,1792]{1,0:T(8,128)(2,1)} %broadcast_select_fusion.1, pred[]{:T(512)S(6)} %eq.32, f32[1,1,1792,1792]{3,2,1,0:T(8,128)} %param.9), kind=kOutput, calls=%fused_computation.12 | convolution fusion | flops 19730923520 | bytes 20185088 | tf_op jit(solution)/shard_map/dot_general | solution.py:40
  313.9 8.1 %add_convert_fusion = bf16[512,1792]{1,0:T(8,128)(2,1)} fusion(bf16[512,1792]{1,0:T(8,128)(2,1)} %collective-permute-done.7, f32[512,1792]{1,0:T(8,128)} %dynamic_update_slice.3, f32[512,1792]{1,0:T(8,128)} %get-tuple-element.16, f32[512,1792]{1,0:T(8,128)} %fusion.4, bf16[512,1792]{1,0:T(8,128)(2,1)} %collective-permute-done.5, pred[]{:T(512)S(6)} %lt.30, ...), kind=kLoop, calls=%fused_computation.1 | loop fusion | flops 11010048 | bytes 23855108 | tf_op jit(solution)/shard_map/convert_element_type | solution.py:73
  322.0 75.4 %all-reduce.5.cloned.1.call-done = bf16[512,1792]{1,0:T(8,128)(2,1)} async-done(((bf16[512,1792]{1,0:T(8,128)(2,1)}), bf16[512,1792]{1,0:T(8,128)(2,1)}) %all-reduce.5.cloned.1.call-update) | async-done | bytes 1835024 | tf_op jit(solution)/shard_map/psum | solution.py:73
  397.4 5.4 %fusion = bf16[1024,1792]{0,1:T(8,128)(2,1)} fusion(bf16[512,1792]{1,0:T(8,128)(2,1)} %all-reduce.5.cloned.1.call-done, bf16[1024,512]{1,0:T(8,128)(2,1)S(1)} %copy-done), kind=kOutput, calls=%fused_computation.5 | convolution fusion | flops 1880883200 | bytes 6553600 | tf_op jit(solution)/shard_map/dot_general | solution.py:74
  402.8 5.9 %copy.10 = bf16[1024,1792]{1,0:T(8,128)(2,1)} copy(bf16[1024,1792]{0,1:T(8,128)(2,1)} %fusion) | data formatting | bytes 7340032 | tf_op jit(solution)/shard_map/convert_element_type | solution.py:74
  (30 shorter events, 5.5 us)
Async XLA Ops:
  6.5 390.9 %copy-start = (bf16[1024,512]{1,0:T(8,128)(2,1)S(1)}, bf16[1024,512]{1,0:T(8,128)(2,1)}, u32[]{:S(2)}) copy-start(bf16[1024,512]{1,0:T(8,128)(2,1)} %param.11) | copy-start | bytes 3145732
  6.5 87.6 %all-reduce.3.cloned.1.call-start = ((), (), s32[]{:S(2)}) async-start(), calls=%async_computation | async-start | bytes 3670016 | tf_op jit(solution)/shard_map/psum | solution.py:32
  10.8 386.6 %all-reduce.5.cloned.1.call-start = ((), (), s32[]{:S(2)}) async-start(), calls=%async_computation.1 | async-start | bytes 3670016 | tf_op jit(solution)/shard_map/psum | solution.py:73
  94.1 37.3 %collective-permute-start = (bf16[512,1792]{1,0:T(8,128)(2,1)}, bf16[512,1792]{1,0:T(8,128)(2,1)}, u32[]{:S(2)}, u32[]{:S(2)}) collective-permute-start(bf16[512,1792]{1,0:T(8,128)(2,1)} %all-reduce.3.cloned.1.call-done), channel_id=1, source_target_pairs={{0,1},{1,2},{2,3},{3,4},{4,5},{5,6},{6,7},{7,8},{8,9},{9,10},{10,1... | collective-permute-start | bytes 5505032 | tf_op jit(solution)/shard_map/ppermute | solution.py:10
  99.7 41.7 %collective-permute-start.3 = (bf16[512,1792]{1,0:T(8,128)(2,1)}, bf16[512,1792]{1,0:T(8,128)(2,1)S(1)}, u32[]{:S(2)}, u32[]{:S(2)}) collective-permute-start(bf16[512,1792]{1,0:T(8,128)(2,1)} %convert_element_type.56), channel_id=1, source_target_pairs={{0,15},{1,0},{2,1},{3,2},{4,3},{5,4},{6,5},{7,6},{8,7},{9,8},{10,9... | collective-permute-start | bytes 5505032 | tf_op jit(solution)/shard_map/ppermute | solution.py:10
  105.0 36.4 %copy-start.1 = (f32[512,1792]{1,0:T(8,128)S(1)}, f32[512,1792]{1,0:T(8,128)}, u32[]{:S(2)}) copy-start(f32[512,1792]{1,0:T(8,128)} %get-tuple-element.17) | copy-start | bytes 11010052
  105.0 96.3 %collective-permute-start.6 = (bf16[512,1792]{1,0:T(8,128)(2,1)}, bf16[512,1792]{1,0:T(8,128)(2,1)}, u32[]{:S(2)}, u32[]{:S(2)}) collective-permute-start(bf16[512,1792]{1,0:T(8,128)(2,1)} %all-reduce.3.cloned.1.call-done), channel_id=1, source_target_pairs={{0,8},{1,9},{2,10},{3,11},{4,12},{5,13},{6,14},{7,15},{8,0},{9,1},... | collective-permute-start | bytes 5505032 | tf_op jit(solution)/shard_map/ppermute | solution.py:16
  134.4 74.1 %collective-permute-start.1 = (bf16[512,1792]{1,0:T(8,128)(2,1)}, bf16[512,1792]{1,0:T(8,128)(2,1)}, u32[]{:S(2)}, u32[]{:S(2)}) collective-permute-start(bf16[512,1792]{1,0:T(8,128)(2,1)} %broadcast_select_fusion), channel_id=1, source_target_pairs={{0,2},{1,3},{2,4},{3,5},{4,6},{5,7},{6,8},{7,9},{8,10},{9,11},{10,... | collective-permute-start | bytes 5505032 | tf_op jit(solution)/shard_map/ppermute | solution.py:10
  141.4 76.5 %copy-start.5 = (bf16[512,1792]{1,0:T(8,128)(2,1)}, bf16[512,1792]{1,0:T(8,128)(2,1)S(1)}, u32[]{:S(2)}) copy-start(bf16[512,1792]{1,0:T(8,128)(2,1)S(1)} %collective-permute-done.3) | copy-start | bytes 5505028
  143.4 74.5 %collective-permute-start.4 = (bf16[512,1792]{1,0:T(8,128)(2,1)}, bf16[512,1792]{1,0:T(8,128)(2,1)}, u32[]{:S(2)}, u32[]{:S(2)}) collective-permute-start(bf16[512,1792]{1,0:T(8,128)(2,1)} %fusion.1), channel_id=1, source_target_pairs={{0,14},{1,15},{2,0},{3,1},{4,2},{5,3},{6,4},{7,5},{8,6},{9,7},{10,... | collective-permute-start | bytes 5505032 | tf_op jit(solution)/shard_map/ppermute | solution.py:10
  208.5 3.2 copy-start.4
  208.5 3.2 copy-start.6
  211.6 82.7 %collective-permute-start.2 = (bf16[512,1792]{1,0:T(8,128)(2,1)}, bf16[512,1792]{1,0:T(8,128)(2,1)}, u32[]{:S(2)}, u32[]{:S(2)}) collective-permute-start(bf16[512,1792]{1,0:T(8,128)(2,1)} %broadcast_select_fusion.1), channel_id=1, source_target_pairs={{0,4},{1,5},{2,6},{3,7},{4,8},{5,9},{6,10},{7,11},{8,12},{9,13},{1... | collective-permute-start | bytes 5505032 | tf_op jit(solution)/shard_map/ppermute | solution.py:10
  211.7 6.3 %copy-start.2 = (f32[512,1792]{1,0:T(8,128)S(1)}, f32[512,1792]{1,0:T(8,128)}, u32[]{:S(2)}) copy-start(f32[512,1792]{1,0:T(8,128)} %get-tuple-element.17) | copy-start | bytes 11010052
  217.1 96.8 %collective-permute-start.7 = (bf16[512,1792]{1,0:T(8,128)(2,1)}, bf16[512,1792]{1,0:T(8,128)(2,1)}, u32[]{:S(2)}, u32[]{:S(2)}) collective-permute-start(bf16[512,1792]{1,0:T(8,128)(2,1)} %get-tuple-element.15), channel_id=1, source_target_pairs={{0,8},{1,9},{2,10},{3,11},{4,12},{5,13},{6,14},{7,15},{8,0},{9,1},... | collective-permute-start | bytes 5505032 | tf_op jit(solution)/shard_map/ppermute | solution.py:16
  221.4 92.5 %collective-permute-start.5 = (bf16[512,1792]{1,0:T(8,128)(2,1)}, bf16[512,1792]{1,0:T(8,128)(2,1)}, u32[]{:S(2)}, u32[]{:S(2)}) collective-permute-start(bf16[512,1792]{1,0:T(8,128)(2,1)} %fusion.8), channel_id=1, source_target_pairs={{0,12},{1,13},{2,14},{3,15},{4,0},{5,1},{6,2},{7,3},{8,4},{9,5},{1... | collective-permute-start | bytes 5505032 | tf_op jit(solution)/shard_map/ppermute | solution.py:10
  294.3 19.6 %copy-start.3 = (f32[512,1792]{1,0:T(8,128)S(1)}, f32[512,1792]{1,0:T(8,128)}, u32[]{:S(2)}) copy-start(f32[512,1792]{1,0:T(8,128)} %get-tuple-element.17) | copy-start | bytes 11010052
Sparse Core Ops, SparseCore 0:
  10.9 83.1 all-reduce.2
  322.1 75.2 all-reduce.4
where the time goes:
time: 416 us
  waiting for transfers between devices  318 us (76%)
  matrix products  36.8 us (9%)
  other arithmetic  24.2 us (6%)
  between operations  13.5 us (3%)
  local copies, waits for them, and re-layouts  11.9 us (3%)
  starting transfers between devices  11.5 us (3%)
    ppermute x6, waiting for transfers between devices, passed_along(): return lax.ppermute(value, axis, pairs)  102 us
    psum x1, waiting for transfers between devices, shards(): own_keys = lax.psum(partial_keys.astype(jnp.bfloat16), 'row')  83.3 us
    psum x1, waiting for transfers between devices, shards(): q_block = lax.psum(summed.astype(jnp.bfloat16), 'row')  75.4 us
    ppermute x2, waiting for transfers between devices, from_partner(): return lax.ppermute(value, axis, pairs)  56.9 us
    dot_general x1, matrix products, shards(): jnp.dot(lagged.astype(jnp.float32), cov_block, precision=highest, preferr...  19.6 us
    ppermute x6, starting transfers between devices, passed_along(): return lax.ppermute(value, axis, pairs)  9.48 us
    convert_element_type x3, other arithmetic, shards(): mirror.astype(jnp.bfloat16)  8.85 us
  transfers between devices with their start and end apart: 10, of which 7 were waited for; matrix products, arithmetic and copies ran while one was open for 12% of the time, Pallas kernels for 0%

commit v1 on v0

v1 whole, which is shorter than its diff:
```python
import functools

import jax
import jax.numpy as jnp
from jax import lax
from jax.experimental import pallas as pl
from jax.experimental.pallas import tpu as pltpu
from jax.sharding import PartitionSpec as P

MESH = pl.DeviceIdType.MESH
F32 = jnp.float32
BF16 = jnp.bfloat16
NX = 4
NROW = 8
NCOL = 16
SLAB = 16


def remote(src, dst, send_sem, recv_sem, row, col):
    return pltpu.make_async_remote_copy(
        src_ref=src,
        dst_ref=dst,
        send_sem=send_sem,
        recv_sem=recv_sem,
        device_id=(row, col),
        device_id_type=MESH,
    )


def add_rows(out_ref, out_at, rows, terms):
    def step(i, carry):
        at = pl.multiple_of(i * SLAB, SLAB)
        total = None
        for ref, start in terms:
            part = ref[pl.ds(pl.multiple_of(start + at, SLAB), SLAB), :].astype(F32)
            total = part if total is None else total + part
        out_ref[pl.ds(pl.multiple_of(out_at + at, SLAB), SLAB), :] = total.astype(out_ref.dtype)
        return carry

    lax.fori_loop(0, rows // SLAB, step, 0)


def kernel(
    edit_ref, tok_ref, cov_ref, far_ref, out_ref,
    counts, part, cov_f, cov, slab_f, slab_send, slab_in, slab_pad,
    own, lag, mir, direct, win, nout_send, nout,
    k_ra1, k_ra2, k_rb1, k_rb2, k_sa, k_sb,
    q_ra1, q_ra2, q_rb1, q_rb2, q_sa, q_sb, m_in, q_sum, q_all,
    cov_sem, slab_sem, loc_sem,
    krs_s, krs_r, kag_s, kag_r, qrs_s, qrs_r, qag_s, qag_r,
    lag_s, lag_r, mir_s, mir_r, far_s, far_r,
):
    r = lax.axis_index("row")
    c = lax.axis_index("col")
    x = r % NX
    yl = r // NX
    ry = (r + NX) % NROW
    edits, width = own.shape
    half = edits // 2
    ch = half // NROW
    tok_dev = tok_ref.shape[0]
    tile = 256
    tiles = width // tile
    far_rows = slab_f.shape[0]

    def across(d):
        return yl * NX + (x + d) % NX

    def lag_col(i):
        return (c + i) % NCOL

    base_col = (c + NCOL - r) % NCOL
    low = c < NCOL // 2
    far_col = (c + NCOL // 2) % NCOL

    def chunk_a(row):
        return pl.multiple_of((row % NX) * (2 * ch) + (row // NX) * ch, ch)

    def chunk_b(row):
        return pl.multiple_of(half + (row // NX) * (NX * ch) + (row % NX) * ch, ch)

    def cov_copy(i):
        rows = pl.ds(i * tile, tile)
        return pltpu.make_async_copy(cov_ref.at[0, 0, rows], cov_f.at[rows], cov_sem.at[i])

    slab_copy = pltpu.make_async_copy(far_ref.at[0], slab_f, slab_sem)
    barrier = pltpu.get_barrier_semaphore()

    def greet(row, col):
        pl.semaphore_signal(barrier, inc=1, device_id=(row, col), device_id_type=MESH)

    for d in range(1, NX):
        greet(across(d), c)
    greet(ry, c)
    greet(r, far_col)

    def greet_lag(i, carry):
        greet(i, lag_col(i))
        return carry

    lax.fori_loop(1, NROW, greet_lag, 0)

    def greet_base(i, carry):
        greet(i, base_col)
        return carry

    @pl.when(r > 0)
    def _():
        lax.fori_loop(0, NROW, greet_base, 0)

    slab_copy.start()
    for i in range(tiles):
        cov_copy(i).start()

    def count_rows(i, carry):
        rows = pl.ds(pl.multiple_of(i * 64, 64), 64)
        relative = edit_ref[rows, :] - r * tok_dev
        slots = lax.broadcasted_iota(jnp.int32, (64, tok_dev), 1)
        total = jnp.zeros((64, tok_dev), F32)
        for j in range(edit_ref.shape[1]):
            total = total + (relative[:, j : j + 1] == slots).astype(F32)
        counts[rows, :] = (total / edit_ref.shape[1]).astype(BF16)
        return carry

    lax.fori_loop(0, edits // 64, count_rows, 0)

    def partial_keys(h):
        def step(n, carry):
            columns = pl.ds(pl.multiple_of(n * tile, tile), tile)
            part[pl.ds(h * half, half), columns] = jnp.dot(
                counts[pl.ds(h * half, half), :], tok_ref[:, columns], preferred_element_type=F32
            ).astype(BF16)
            return carry

        lax.fori_loop(0, tiles, step, 0)

    def rs_a1(src, ra1, ss, rs, d):
        rows = pl.ds(pl.multiple_of(((x + d) % NX) * (2 * ch), 2 * ch), 2 * ch)
        return remote(src.at[rows], ra1.at[d - 1], ss.at[d - 1], rs.at[d - 1], across(d), c)

    def rs_b1(src, rb1, ss, rs):
        rows = pl.ds(pl.multiple_of(half + (1 - yl) * (NX * ch), NX * ch), NX * ch)
        return remote(src.at[rows], rb1, ss.at[3], rs.at[3], ry, c)

    def rs_a2(sa, ra2, ss, rs):
        rows = pl.ds(pl.multiple_of((1 - yl) * ch, ch), ch)
        return remote(sa.at[rows], ra2, ss.at[4], rs.at[4], ry, c)

    def rs_b2(sb, rb2, ss, rs, d):
        rows = pl.ds(pl.multiple_of(((x + d) % NX) * ch, ch), ch)
        return remote(sb.at[rows], rb2.at[d - 1], ss.at[4 + d], rs.at[4 + d], across(d), c)

    def rs_middle(src, ra1, ra2, rb1, rb2, sa, sb, ss, rs):
        rs_b1(src, rb1, ss, rs).wait_recv()
        add_rows(sb, 0, NX * ch, [(src, half + yl * (NX * ch)), (rb1, 0)])
        for d in range(1, NX):
            rs_b2(sb, rb2, ss, rs, d).start()
        for d in range(1, NX):
            rs_a1(src, ra1, ss, rs, d).wait_recv()
        add_rows(sa, 0, 2 * ch, [(src, x * (2 * ch))] + [(ra1.at[d], 0) for d in range(NX - 1)])
        rs_a2(sa, ra2, ss, rs).start()

    def rs_end(ra2, rb2, sa, sb, ss, rs, out, a_more, b_more):
        rs_a2(sa, ra2, ss, rs).wait_recv()
        add_rows(out, chunk_a(r), ch, [(sa, yl * ch), (ra2, 0)] + a_more)
        for d in range(1, NX):
            rs_b2(sb, rb2, ss, rs, d).wait_recv()
        add_rows(out, chunk_b(r), ch, [(sb, x * ch)] + [(rb2.at[d], 0) for d in range(NX - 1)] + b_more)

    def rs_sent(src, ra1, ra2, rb1, rb2, sa, sb, ss, rs):
        rs_b1(src, rb1, ss, rs).wait_send()
        rs_a2(sa, ra2, ss, rs).wait_send()
        for d in range(1, NX):
            rs_a1(src, ra1, ss, rs, d).wait_send()
            rs_b2(sb, rb2, ss, rs, d).wait_send()

    def ag_a1(full, ss, rs, row):
        rows = pl.ds(chunk_a(row), ch)
        return remote(full.at[rows], full.at[rows], ss.at[0], rs.at[0], ry, c)

    def ag_b1(full, ss, rs, row, d):
        rows = pl.ds(chunk_b(row), ch)
        return remote(full.at[rows], full.at[rows], ss.at[d], rs.at[d], across(d), c)

    def ag_a2(full, ss, rs, xx, d):
        rows = pl.ds(pl.multiple_of(xx * (2 * ch), 2 * ch), 2 * ch)
        return remote(full.at[rows], full.at[rows], ss.at[3 + d], rs.at[3 + d], across(d), c)

    def ag_b2(full, ss, rs, yy):
        rows = pl.ds(pl.multiple_of(half + yy * (NX * ch), NX * ch), NX * ch)
        return remote(full.at[rows], full.at[rows], ss.at[7], rs.at[7], ry, c)

    def ag_start(full, ss, rs):
        ag_a1(full, ss, rs, r).start()
        for d in range(1, NX):
            ag_b1(full, ss, rs, r, d).start()

    def behind(d):
        return (x + NX - d) % NX

    def ag_middle(full, ss, rs):
        ag_a1(full, ss, rs, ry).wait_recv()
        for d in range(1, NX):
            ag_a2(full, ss, rs, x, d).start()
        for d in range(1, NX):
            ag_b1(full, ss, rs, yl * NX + behind(d), d).wait_recv()
        ag_b2(full, ss, rs, yl).start()

    def ag_end(full, ss, rs):
        for d in range(1, NX):
            ag_a2(full, ss, rs, behind(d), d).wait_recv()
        ag_b2(full, ss, rs, 1 - yl).wait_recv()

    def ag_sent(full, ss, rs):
        ag_a1(full, ss, rs, r).wait_send()
        for d in range(1, NX):
            ag_b1(full, ss, rs, r, d).wait_send()
            ag_a2(full, ss, rs, x, d).wait_send()
        ag_b2(full, ss, rs, yl).wait_send()

    def lag_copy(h, source, i):
        rows = pl.ds((chunk_a if h == 0 else chunk_b)(source), ch)
        return remote(
            own.at[rows], lag.at[rows], lag_s.at[i, h], lag_r.at[source, h], i, lag_col(i)
        )

    def mir_copy(h, e, slot):
        rows = pl.ds((chunk_a if h == 0 else chunk_b)(e), ch)
        return remote(
            mir.at[rows], m_in.at[slot, h], mir_s.at[e, h], mir_r.at[slot, h], e, base_col
        )

    def each(low_end, high_end, do):
        def step(i, carry):
            do(i)
            return carry

        lax.fori_loop(low_end, high_end, step, 0)

    at_0 = r * far_rows
    at_1 = width // 2 + r * far_rows
    start_0 = pl.multiple_of(at_0 // 128 * 128, 128)
    start_1 = pl.multiple_of(jnp.minimum(at_1 // 128 * 128, width - tile), 128)

    def slab_far():
        return remote(slab_send, slab_in, far_s.at[0], far_r.at[0], r, far_col)

    def win_far(h):
        columns = pl.ds(start_0 if h == 0 else start_1, tile)
        return remote(
            own.at[:, columns], win.at[:, pl.ds(h * tile, tile)], far_s.at[1 + h], far_r.at[1 + h], r, far_col
        )

    def nout_far():
        return remote(nout_send, nout, far_s.at[3], far_r.at[3], r, far_col)

    krs = (part, k_ra1, k_ra2, k_rb1, k_rb2, k_sa, k_sb, krs_s, krs_r)
    qrs = (direct, q_ra1, q_ra2, q_rb1, q_rb2, q_sa, q_sb, qrs_s, qrs_r)

    partial_keys(0)
    pl.semaphore_wait(barrier, 5 + NROW - 1 + jnp.where(r > 0, NROW, 0))
    for d in range(1, NX):
        rs_a1(part, k_ra1, krs_s, krs_r, d).start()
    partial_keys(1)
    rs_b1(part, k_rb1, krs_s, krs_r).start()

    slab_copy.wait()

    @pl.when(low)
    def _():
        add_rows(slab_send, 0, far_rows, [(slab_f, 0)])
        slab_far().start()

    for i in range(tiles):
        cov_copy(i).wait()
        add_rows(cov, i * tile, tile, [(cov_f, i * tile)])

    @pl.when(jnp.logical_not(low))
    def _():
        slab_pad[...] = jnp.zeros_like(slab_pad)
        add_rows(slab_pad, tile + at_1 - start_1, far_rows, [(slab_f, 0)])

    rs_middle(*krs)
    rs_end(k_ra2, k_rb2, k_sa, k_sb, krs_s, krs_r, own, [], [])
    ag_start(own, kag_s, kag_r)
    ag_middle(own, kag_s, kag_r)

    def send_lag(i):
        lag_copy(0, r, i).start()
        lag_copy(1, r, i).start()

    each(1, NROW, send_lag)

    @pl.when(jnp.logical_not(low))
    def _():
        slab_far().wait_recv()
        add_rows(slab_pad, at_0 - start_0, far_rows, [(slab_in, 0)])

    ag_end(own, kag_s, kag_r)

    @pl.when(low)
    def _():
        win_far(0).start()
        win_far(1).start()

    contract_last = (((1,), (1,)), ((), ()))

    @pl.when(r > 0)
    def _():
        def mirror(n):
            block = pl.ds(pl.multiple_of(n * tile, tile), tile)
            mir[:, block] = lax.dot_general(
                own[...], cov[block, :], contract_last, preferred_element_type=F32
            ).astype(BF16)

        each(0, tiles, mirror)

        def send_mir(e):
            mir_copy(0, e, r - 1).start()
            mir_copy(1, e, r - 1).start()

        each(0, NROW, send_mir)

    @pl.when(jnp.logical_not(low))
    def _():
        def narrow(n):
            block = pl.ds(pl.multiple_of(n * tile, tile), tile)
            nout_send[:, block] = lax.dot_general(
                own[...], slab_pad[block, :], contract_last, preferred_element_type=F32
            ).astype(BF16)

        each(0, 2, narrow)
        nout_far().start()

    own_to_lag = pltpu.make_async_copy(own, lag, loc_sem)

    @pl.when(r == 0)
    def _():
        own_to_lag.start()
        own_to_lag.wait()

    @pl.when(r > 0)
    def _():
        def got_lag(e):
            lag_copy(0, e, 0).wait_recv()
            lag_copy(1, e, 0).wait_recv()

        each(0, NROW, got_lag)

    @pl.when(low)
    def _():
        def step(n):
            block = pl.ds(pl.multiple_of(n * tile, tile), tile)
            direct[:, block] = jnp.dot(
                lag[...], cov[:, block], preferred_element_type=F32
            ).astype(BF16)

        each(0, tiles, step)
        nout_far().wait_recv()

        def add_narrow(i):
            rows = pl.ds(pl.multiple_of(i * 64, 64), 64)
            for h, start in ((0, start_0), (1, start_1)):
                columns = pl.ds(start, tile)
                direct[rows, columns] = (
                    direct[rows, columns].astype(F32)
                    + nout[rows, pl.ds(h * tile, tile)].astype(F32)
                ).astype(BF16)

        each(0, edits // 64, add_narrow)

    @pl.when(jnp.logical_not(low))
    def _():
        win_far(0).wait_recv()
        win_far(1).wait_recv()

        def step(n):
            block = pl.ds(pl.multiple_of(n * tile, tile), tile)
            direct[:, block] = (
                jnp.dot(lag[...], cov[:, block], preferred_element_type=F32)
                + jnp.dot(win[...], slab_pad[:, block], preferred_element_type=F32)
            ).astype(BF16)

        each(0, tiles, step)

    for d in range(1, NX):
        rs_a1(direct, q_ra1, qrs_s, qrs_r, d).start()
    rs_b1(direct, q_rb1, qrs_s, qrs_r).start()
    rs_middle(*qrs)

    def got_mir(i):
        mir_copy(0, r, i).wait_recv()
        mir_copy(1, r, i).wait_recv()

    each(0, NROW - 1, got_mir)
    for h in range(2):
        add_rows(q_sum, h * ch, ch, [(m_in.at[i, h], 0) for i in range(NROW - 1)])
    rs_end(q_ra2, q_rb2, q_sa, q_sb, qrs_s, qrs_r, q_all, [(q_sum, 0)], [(q_sum, ch)])
    ag_start(q_all, qag_s, qag_r)
    ag_middle(q_all, qag_s, qag_r)
    ag_end(q_all, qag_s, qag_r)
    result = pltpu.make_async_copy(q_all, out_ref, loc_sem)
    result.start()

    rs_sent(*krs)
    rs_sent(*qrs)
    ag_sent(own, kag_s, kag_r)
    ag_sent(q_all, qag_s, qag_r)

    def lag_sent(i):
        lag_copy(0, r, i).wait_send()
        lag_copy(1, r, i).wait_send()

    each(1, NROW, lag_sent)

    @pl.when(r > 0)
    def _():
        def mir_sent(e):
            mir_copy(0, e, r - 1).wait_send()
            mir_copy(1, e, r - 1).wait_send()

        each(0, NROW, mir_sent)

    @pl.when(low)
    def _():
        slab_far().wait_send()
        win_far(0).wait_send()
        win_far(1).wait_send()

    @pl.when(jnp.logical_not(low))
    def _():
        nout_far().wait_send()

    result.wait()


def delta_kernel(residual_ref, q_ref, out_ref):
    out_ref[...] = jnp.dot(residual_ref[...], q_ref[...], preferred_element_type=F32).astype(
        out_ref.dtype
    )


def shards(tokens, edit_src, cov_tiles, cov_far, residual):
    edits = edit_src.shape[0]
    tok_dev, width = tokens.shape
    ch = edits // 2 // NROW
    far_rows = cov_far.shape[1]
    tiles = width // 256

    def buf(*shape, dtype=BF16):
        return pltpu.VMEM(shape, dtype)

    def dma(*shape):
        return pltpu.SemaphoreType.DMA(shape)

    def reduce_bufs():
        return [
            buf(NX - 1, 2 * ch, width), buf(ch, width), buf(NX * ch, width),
            buf(NX - 1, ch, width), buf(2 * ch, width), buf(NX * ch, width),
        ]

    q_block = pl.pallas_call(
        kernel,
        name="edit_product",
        out_shape=jax.ShapeDtypeStruct((edits, width), BF16),
        in_specs=[
            pl.BlockSpec(memory_space=pltpu.VMEM),
            pl.BlockSpec(memory_space=pltpu.VMEM),
            pl.BlockSpec(memory_space=pl.ANY),
            pl.BlockSpec(memory_space=pl.ANY),
        ],
        out_specs=pl.BlockSpec(memory_space=pl.ANY),
        scratch_shapes=[
            buf(edits, tok_dev), buf(edits, width),
            buf(width, width, dtype=F32), buf(width, width),
            buf(far_rows, width, dtype=F32), buf(far_rows, width), buf(far_rows, width), buf(512, width),
            buf(edits, width), buf(edits, width), buf(edits, width), buf(edits, width),
            buf(edits, 512), buf(edits, 512), buf(edits, 512),
            *reduce_bufs(),
            *reduce_bufs(),
            buf(NROW - 1, 2, ch, width), buf(2 * ch, width, dtype=F32), buf(edits, width),
            dma(tiles), pltpu.SemaphoreType.DMA, pltpu.SemaphoreType.DMA,
            dma(8), dma(8), dma(8), dma(8), dma(8), dma(8), dma(8), dma(8),
            dma(NROW, 2), dma(NROW, 2), dma(NROW, 2), dma(NROW - 1, 2), dma(4), dma(4),
        ],
        compiler_params=pltpu.CompilerParams(
            collective_id=0, has_side_effects=True, vmem_limit_bytes=60 * 2**20
        ),
    )(edit_src, tokens, cov_tiles, cov_far)

    rows = residual.shape[0]
    step = 256
    return pl.pallas_call(
        delta_kernel,
        name="delta",
        grid=(rows // step,),
        out_shape=jax.ShapeDtypeStruct((rows, width), BF16),
        in_specs=[
            pl.BlockSpec((step, edits), lambda i: (i, 0)),
            pl.BlockSpec((edits, width), lambda i: (0, 0)),
        ],
        out_specs=pl.BlockSpec((step, width), lambda i: (i, 0)),
        compiler_params=pltpu.CompilerParams(vmem_limit_bytes=32 * 2**20),
    )(residual, q_block)


def solution(mesh):
    placed = (
        P("row", "col"),
        P(),
        P("row", "col", None, None),
        P("col", "row", None),
        P("row", None),
    )
    return jax.shard_map(
        shards, mesh=mesh, in_specs=placed, out_specs=P("row", "col"), check_vma=False
    )
```

time: 416 us -> 168 us (0.40)
  the two profiles are of different devices: /device:TPU:0 before, /device:TPU:32 now
where the time goes in v1:
time: 168 us
  Pallas kernels  165 us (98%)
  local copies, waits for them, and re-layouts  3.05 us (2%)
    pallas_call x1, Pallas kernels, shards(): pl.pallas_call(kernel, name='edit_product', out_shape=jax.ShapeDtypeStruc...  161 us
    pallas_call x1, Pallas kernels, shards(): pl.pallas_call(delta_kernel, name='delta', grid=(rows // step,), out_shap...  3.79 us

profile of v1, /device:TPU:32, one launch (start us, length us, event | category | flops | bytes accessed | tf_op | source)
XLA Modules:
  0.0 167.9 jit_solution(12310595311100394746)
XLA Ops:
  0.0 1.5 copy.6.edit_ref
  1.6 0.0 copy-start.1
  1.6 161.1 %edit_product.1.q_ref = bf16[512,1792]{1,0:T(8,128)(2,1)} custom-call(s32[512,4]{1,0:T(8,128)} %copy.6.edit_ref, bf16[256,1792]{1,0:T(8,128)(2,1)} %tok_ref.1, f32[1,1,1792,1792]{3,2,1,0:T(8,128)} %cov_ref.1, f32[1,112,1792]{2,1,0:T(8,128)} %far_ref.1), custom_call_target="tpu_custom_call" | custom-call | tf_op jit(solution)/shard_map/edit_product/pallas_call | solution.py:462
  162.6 0.0 copy-done.1
  162.6 0.0 copy-start
  162.7 1.5 copy-done
  164.1 3.8 %delta.1 = bf16[1024,1792]{1,0:T(8,128)(2,1)} custom-call(bf16[1024,512]{1,0:T(8,128)(2,1)S(1)} %copy-done.1, bf16[512,1792]{1,0:T(8,128)(2,1)S(1)} %copy-done), custom_call_target="tpu_custom_call" | custom-call | tf_op jit(solution)/shard_map/delta/pallas_call | solution.py:493
Async XLA Ops:
  1.6 161.1 %copy-start.1 = (bf16[1024,512]{1,0:T(8,128)(2,1)S(1)}, bf16[1024,512]{1,0:T(8,128)(2,1)}, u32[]{:S(2)}) copy-start(bf16[1024,512]{1,0:T(8,128)(2,1)} %residual_ref.1) | copy-start | bytes 3145732
  162.6 1.5 copy-start

commit v2 on v1

--- a/solution.py
+++ b/solution.py
@@ -13,6 +13,7 @@
 NX = 4
 NROW = 8
 NCOL = 16
+PLANE = 4
 SLAB = 16
 
 
@@ -45,10 +46,10 @@
     counts, part, cov_f, cov, slab_f, slab_send, slab_in, slab_pad,
     own, lag, mir, direct, win, nout_send, nout,
     k_ra1, k_ra2, k_rb1, k_rb2, k_sa, k_sb,
-    q_ra1, q_ra2, q_rb1, q_rb2, q_sa, q_sb, m_in, q_sum, q_all,
+    q_ra1, q_ra2, q_rb1, q_rb2, q_sa, q_sb, m_in, q_sum, q_all, relay, crossed, cross_in,
     cov_sem, slab_sem, loc_sem,
     krs_s, krs_r, kag_s, kag_r, qrs_s, qrs_r, qag_s, qag_r,
-    lag_s, lag_r, mir_s, mir_r, far_s, far_r,
+    lag_s, lag_r, mir_s, mir_r, far_s, far_r, rel_s, rel_r, cross_s, cross_r, stay_sem,
 ):
     r = lax.axis_index("row")
     c = lax.axis_index("col")
@@ -66,10 +67,16 @@
     def across(d):
         return yl * NX + (x + d) % NX
 
-    def lag_col(i):
-        return (c + i) % NCOL
-
-    base_col = (c + NCOL - r) % NCOL
+    u = c % PLANE
+    plane = c - u
+    is_mid = r == PLANE
+
+    def ahead(i):
+        return plane + (u + i) % PLANE
+
+    source_col = plane + (u + NCOL - r) % PLANE
+    up_col = (c + PLANE) % NCOL
+    down_col = (c + NCOL - PLANE) % NCOL
     low = c < NCOL // 2
     far_col = (c + NCOL // 2) % NCOL
 
@@ -93,20 +100,29 @@
         greet(across(d), c)
     greet(ry, c)
     greet(r, far_col)
-
-    def greet_lag(i, carry):
-        greet(i, lag_col(i))
-        return carry
-
-    lax.fori_loop(1, NROW, greet_lag, 0)
-
-    def greet_base(i, carry):
-        greet(i, base_col)
-        return carry
+    greet(r, up_col)
+    greet(r, down_col)
+
+    def each(low_end, high_end, do):
+        def step(i, carry):
+            do(i)
+            return carry
+
+        lax.fori_loop(low_end, high_end, step, 0)
+
+    def others(low_end, high_end, do):
+        def step(i):
+            @pl.when(jnp.logical_not(jnp.logical_and(is_mid, i == PLANE)))
+            def _():
+                do(i)
+
+        each(low_end, high_end, step)
+
+    others(1, NROW, lambda i: greet(i, ahead(i)))
 
     @pl.when(r > 0)
     def _():
-        lax.fori_loop(0, NROW, greet_base, 0)
+        others(0, NROW, lambda e: greet(e, source_col))
 
     slab_copy.start()
     for i in range(tiles):
@@ -218,24 +234,50 @@
             ag_a2(full, ss, rs, x, d).wait_send()
         ag_b2(full, ss, rs, yl).wait_send()
 
-    def lag_copy(h, source, i):
-        rows = pl.ds((chunk_a if h == 0 else chunk_b)(source), ch)
+    def chunk(h, row):
+        return pl.ds((chunk_a if h == 0 else chunk_b)(row), ch)
+
+    def relay_copy(h, far):
         return remote(
-            own.at[rows], lag.at[rows], lag_s.at[i, h], lag_r.at[source, h], i, lag_col(i)
+            own.at[chunk(h, r)], relay.at[far, h], rel_s.at[far, h], rel_r.at[far, h], r,
+            far_col if far else up_col,
         )
 
+    def lag_copy(h, source, i, held):
+        return remote(
+            held, lag.at[chunk(h, source)], lag_s.at[i, h], lag_r.at[source, h], i, ahead(i)
+        )
+
+    def lag_stay(h, held):
+        return pltpu.make_async_copy(held, lag.at[chunk(h, r)], stay_sem.at[h])
+
     def mir_copy(h, e, slot):
-        rows = pl.ds((chunk_a if h == 0 else chunk_b)(e), ch)
         return remote(
-            mir.at[rows], m_in.at[slot, h], mir_s.at[e, h], mir_r.at[slot, h], e, base_col
+            mir.at[chunk(h, e)], m_in.at[slot, h], mir_s.at[e, h], mir_r.at[slot, h], e, source_col
         )
 
-    def each(low_end, high_end, do):
-        def step(i, carry):
-            do(i)
-            return carry
-
-        lax.fori_loop(low_end, high_end, step, 0)
+    def mir_stay(h):
+        return pltpu.make_async_copy(mir.at[chunk(h, r)], m_in.at[PLANE - 1, h], stay_sem.at[2 + h])
+
+    def cross_copy(far):
+        return remote(
+            crossed.at[far], cross_in.at[far], cross_s.at[far], cross_r.at[far], r,
+            far_col if far else down_col,
+        )
+
+    def add_slots(out, out_at, first, last):
+        for h in range(2):
+            def step(i, carry):
+                rows = pl.ds(pl.multiple_of(i * SLAB, SLAB), SLAB)
+                total = lax.fori_loop(
+                    first, last,
+                    lambda slot, so_far: so_far + m_in[slot, h, rows, :].astype(F32),
+                    jnp.zeros((SLAB, width), F32),
+                )
+                out[pl.ds(pl.multiple_of(out_at + h * ch + i * SLAB, SLAB), SLAB), :] = total.astype(out.dtype)
+                return carry
+
+            lax.fori_loop(0, ch // SLAB, step, 0)
 
     at_0 = r * far_rows
     at_1 = width // 2 + r * far_rows
@@ -258,7 +300,7 @@
     qrs = (direct, q_ra1, q_ra2, q_rb1, q_rb2, q_sa, q_sb, qrs_s, qrs_r)
 
     partial_keys(0)
-    pl.semaphore_wait(barrier, 5 + NROW - 1 + jnp.where(r > 0, NROW, 0))
+    pl.semaphore_wait(barrier, 14 + jnp.where(r > 0, NROW, 0) - jnp.where(is_mid, 2, 0))
     for d in range(1, NX):
         rs_a1(part, k_ra1, krs_s, krs_r, d).start()
     partial_keys(1)
@@ -282,14 +324,43 @@
 
     rs_middle(*krs)
     rs_end(k_ra2, k_rb2, k_sa, k_sb, krs_s, krs_r, own, [], [])
+    for h in range(2):
+        relay_copy(h, 0).start()
+
+    @pl.when(u > 0)
+    def _():
+        for h in range(2):
+            relay_copy(h, 1).start()
+
     ag_start(own, kag_s, kag_r)
     ag_middle(own, kag_s, kag_r)
 
-    def send_lag(i):
-        lag_copy(0, r, i).start()
-        lag_copy(1, r, i).start()
-
-    each(1, NROW, send_lag)
+    def own_on(i):
+        for h in range(2):
+            lag_copy(h, r, i, own.at[chunk(h, r)]).start()
+
+    def relay_on(far):
+        def send(i):
+            for h in range(2):
+                lag_copy(h, r, i, relay.at[far, h]).start()
+
+        return send
+
+    each(1, PLANE - u, own_on)
+    for h in range(2):
+        relay_copy(h, 0).wait_recv()
+    others(PLANE - u, 2 * PLANE - u, relay_on(0))
+
+    @pl.when(is_mid)
+    def _():
+        for h in range(2):
+            lag_stay(h, relay.at[0, h]).start()
+
+    @pl.when(u > 0)
+    def _():
+        for h in range(2):
+            relay_copy(h, 1).wait_recv()
+        each(2 * PLANE - u, NROW, relay_on(1))
 
     @pl.when(jnp.logical_not(low))
     def _():
@@ -316,10 +387,15 @@
         each(0, tiles, mirror)
 
         def send_mir(e):
-            mir_copy(0, e, r - 1).start()
-            mir_copy(1, e, r - 1).start()
-
-        each(0, NROW, send_mir)
+            for h in range(2):
+                mir_copy(h, e, r - 1).start()
+
+        others(0, NROW, send_mir)
+
+    @pl.when(is_mid)
+    def _():
+        for h in range(2):
+            mir_stay(h).start()
 
     @pl.when(jnp.logical_not(low))
     def _():
@@ -342,10 +418,15 @@
     @pl.when(r > 0)
     def _():
         def got_lag(e):
-            lag_copy(0, e, 0).wait_recv()
-            lag_copy(1, e, 0).wait_recv()
-
-        each(0, NROW, got_lag)
+            for h in range(2):
+                lag_copy(h, e, 1, own.at[chunk(h, r)]).wait_recv()
+
+        others(0, NROW, got_lag)
+
+    @pl.when(is_mid)
+    def _():
+        for h in range(2):
+            lag_stay(h, relay.at[0, h]).wait()
 
     @pl.when(low)
     def _():
@@ -386,15 +467,36 @@
     for d in range(1, NX):
         rs_a1(direct, q_ra1, qrs_s, qrs_r, d).start()
     rs_b1(direct, q_rb1, qrs_s, qrs_r).start()
+
+    def got_mir(i):
+        for h in range(2):
+            mir_copy(h, r, i - 1).wait_recv()
+
+    others(1, NROW, got_mir)
+
+    @pl.when(is_mid)
+    def _():
+        for h in range(2):
+            mir_stay(h).wait()
+
+    add_slots(crossed.at[0], 0, PLANE - u - 1, 2 * PLANE - u - 1)
+    cross_copy(0).start()
+
+    @pl.when(u > 0)
+    def _():
+        add_slots(crossed.at[1], 0, 2 * PLANE - u - 1, NROW - 1)
+        cross_copy(1).start()
+
+    add_slots(q_sum, 0, 0, PLANE - u - 1)
     rs_middle(*qrs)
-
-    def got_mir(i):
-        mir_copy(0, r, i).wait_recv()
-        mir_copy(1, r, i).wait_recv()
-
-    each(0, NROW - 1, got_mir)
-    for h in range(2):
-        add_rows(q_sum, h * ch, ch, [(m_in.at[i, h], 0) for i in range(NROW - 1)])
+    cross_copy(0).wait_recv()
+    add_rows(q_sum, 0, 2 * ch, [(q_sum, 0), (cross_in.at[0], 0)])
+
+    @pl.when(u > 0)
+    def _():
+        cross_copy(1).wait_recv()
+        add_rows(q_sum, 0, 2 * ch, [(q_sum, 0), (cross_in.at[1], 0)])
+
     rs_end(q_ra2, q_rb2, q_sa, q_sb, qrs_s, qrs_r, q_all, [(q_sum, 0)], [(q_sum, ch)])
     ag_start(q_all, qag_s, qag_r)
     ag_middle(q_all, qag_s, qag_r)
@@ -408,18 +510,28 @@
     ag_sent(q_all, qag_s, qag_r)
 
     def lag_sent(i):
-        lag_copy(0, r, i).wait_send()
-        lag_copy(1, r, i).wait_send()
-
-    each(1, NROW, lag_sent)
+        for h in range(2):
+            lag_copy(h, r, i, own.at[chunk(h, r)]).wait_send()
+
+    others(1, NROW, lag_sent)
 
     @pl.when(r > 0)
     def _():
         def mir_sent(e):
-            mir_copy(0, e, r - 1).wait_send()
-            mir_copy(1, e, r - 1).wait_send()
-
-        each(0, NROW, mir_sent)
+            for h in range(2):
+                mir_copy(h, e, r - 1).wait_send()
+
+        others(0, NROW, mir_sent)
+
+    for h in range(2):
+        relay_copy(h, 0).wait_send()
+    cross_copy(0).wait_send()
+
+    @pl.when(u > 0)
+    def _():
+        for h in range(2):
+            relay_copy(h, 1).wait_send()
+        cross_copy(1).wait_send()
 
     @pl.when(low)
     def _():
@@ -479,9 +591,11 @@
             *reduce_bufs(),
             *reduce_bufs(),
             buf(NROW - 1, 2, ch, width), buf(2 * ch, width, dtype=F32), buf(edits, width),
+            buf(2, 2, ch, width), buf(2, 2 * ch, width), buf(2, 2 * ch, width),
             dma(tiles), pltpu.SemaphoreType.DMA, pltpu.SemaphoreType.DMA,
             dma(8), dma(8), dma(8), dma(8), dma(8), dma(8), dma(8), dma(8),
             dma(NROW, 2), dma(NROW, 2), dma(NROW, 2), dma(NROW - 1, 2), dma(4), dma(4),
+            dma(2, 2), dma(2, 2), dma(2), dma(2), dma(4),
         ],
         compiler_params=pltpu.CompilerParams(
             collective_id=0, has_side_effects=True, vmem_limit_bytes=60 * 2**20

time: 168 us -> 149 us (0.89)
  the two profiles are of different devices: /device:TPU:32 before, /device:TPU:0 now
where the time goes in v2:
time: 149 us; the launch traced here: 147 us
  Pallas kernels  144 us (97%)
  local copies, waits for them, and re-layouts  3.05 us (2%)
    pallas_call x1, Pallas kernels, shards(): pl.pallas_call(kernel, name='edit_product', out_shape=jax.ShapeDtypeStruc...  141 us
    pallas_call x1, Pallas kernels, shards(): pl.pallas_call(delta_kernel, name='delta', grid=(rows // step,), out_shap...  3.79 us
    unnamed x5, local copies, waits for them, and re-layouts  3.05 us

profile of v2, /device:TPU:0, one launch (start us, length us, event | category | flops | bytes accessed | tf_op | source)
XLA Modules:
  0.0 147.4 jit_solution(5823993648521603657)
XLA Ops:
  0.0 1.5 %copy.6.edit_ref = s32[512,4]{1,0:T(8,128)} copy(s32[512,4]{0,1:T(4,128)} %param.6) | data formatting | bytes 16384 | tf_op args[1]
  1.6 0.0 copy-start.1
  1.6 140.5 %edit_product.1.q_ref = bf16[512,1792]{1,0:T(8,128)(2,1)} custom-call(s32[512,4]{1,0:T(8,128)} %copy.6.edit_ref, bf16[256,1792]{1,0:T(8,128)(2,1)} %tok_ref.1, f32[1,1,1792,1792]{3,2,1,0:T(8,128)} %cov_ref.1, f32[1,112,1792]{2,1,0:T(8,128)} %far_ref.1), custom_call_target="tpu_custom_call" | custom-call | tf_op jit(solution)/shard_map/edit_product/pallas_call | solution.py:574
  142.1 0.0 copy-done.1
  142.1 0.0 copy-start
  142.1 1.5 %copy-done = bf16[512,1792]{1,0:T(8,128)(2,1)S(1)} copy-done((bf16[512,1792]{1,0:T(8,128)(2,1)S(1)}, bf16[512,1792]{1,0:T(8,128)(2,1)}, u32[]{:S(2)}) %copy-start) | copy-done | bytes 1835032
  143.6 3.8 %delta.1 = bf16[1024,1792]{1,0:T(8,128)(2,1)} custom-call(bf16[1024,512]{1,0:T(8,128)(2,1)S(1)} %copy-done.1, bf16[512,1792]{1,0:T(8,128)(2,1)S(1)} %copy-done), custom_call_target="tpu_custom_call" | custom-call | tf_op jit(solution)/shard_map/delta/pallas_call | solution.py:607
Async XLA Ops:
  1.6 140.5 %copy-start.1 = (bf16[1024,512]{1,0:T(8,128)(2,1)S(1)}, bf16[1024,512]{1,0:T(8,128)(2,1)}, u32[]{:S(2)}) copy-start(bf16[1024,512]{1,0:T(8,128)(2,1)} %residual_ref.1) | copy-start | bytes 3145732
  142.1 1.5 %copy-start = (bf16[512,1792]{1,0:T(8,128)(2,1)S(1)}, bf16[512,1792]{1,0:T(8,128)(2,1)}, u32[]{:S(2)}) copy-start(bf16[512,1792]{1,0:T(8,128)(2,1)} %edit_product.1.q_ref) | copy-start | bytes 5505028

commit v3 on v0

v3 whole, which is shorter than its diff:
```python
import functools

import jax
import jax.numpy as jnp
from jax import lax
from jax.experimental import pallas as pl
from jax.experimental.pallas import tpu as pltpu
from jax.sharding import PartitionSpec as P

MESH = pl.DeviceIdType.MESH
F32 = jnp.float32
BF16 = jnp.bfloat16
NX = 4
NROW = 8
NCOL = 16
PLANE = 4
GROUPS = 2
SLAB = 16


def remote(src, dst, send_sem, recv_sem, row, col):
    return pltpu.make_async_remote_copy(
        src_ref=src,
        dst_ref=dst,
        send_sem=send_sem,
        recv_sem=recv_sem,
        device_id=(row, col),
        device_id_type=MESH,
    )


def add_rows(out_ref, out_at, rows, terms):
    def step(i, carry):
        at = pl.multiple_of(i * SLAB, SLAB)
        total = None
        for ref, start in terms:
            part = ref[pl.ds(pl.multiple_of(start + at, SLAB), SLAB), :].astype(F32)
            total = part if total is None else total + part
        out_ref[pl.ds(pl.multiple_of(out_at + at, SLAB), SLAB), :] = total.astype(out_ref.dtype)
        return carry

    lax.fori_loop(0, rows // SLAB, step, 0)


def kernel(
    edit_ref, tok_ref, cov_ref, far_ref, out_ref,
    counts, part, cov_f, cov, slab_f, slab_send, slab_in, slab_pad,
    own, lag, mir, direct, win, nout_send, nout,
    k_ra1, k_ra2, k_rb1, k_rb2, k_sa, k_sb,
    q_ra1, q_ra2, q_rb1, q_rb2, q_sa, q_sb, m_in, q_sum, q_all, relay, crossed, cross_in,
    cov_sem, slab_sem, loc_sem, out_sem,
    krs_s, krs_r, kag_s, kag_r, qrs_s, qrs_r, qag_s, qag_r,
    lag_s, lag_r, mir_s, mir_r, slab_s, slab_r, win_s, win_r, nout_s, nout_r,
    rel_s, rel_r, cross_s, cross_r, stay_sem,
):
    r = lax.axis_index("row")
    c = lax.axis_index("col")
    x = r % NX
    yl = r // NX
    ry = (r + NX) % NROW
    edits, width = own.shape
    group = edits // GROUPS
    half = group // 2
    ch = half // NROW
    tok_dev = tok_ref.shape[0]
    tile = 256
    tiles = width // tile
    far_rows = slab_f.shape[0]
    groups = range(GROUPS)

    def across(d):
        return yl * NX + (x + d) % NX

    def behind(d):
        return (x + NX - d) % NX

    u = c % PLANE
    plane = c - u
    is_mid = r == PLANE

    def ahead(i):
        return plane + (u + i) % PLANE

    source_col = plane + (u + NCOL - r) % PLANE
    up_col = (c + PLANE) % NCOL
    down_col = (c + NCOL - PLANE) % NCOL
    low = c < NCOL // 2
    far_col = (c + NCOL // 2) % NCOL

    def chunk_at(g, h, row):
        if h == 0:
            at = (row % NX) * (2 * ch) + (row // NX) * ch
        else:
            at = half + (row // NX) * (NX * ch) + (row % NX) * ch
        return pl.multiple_of(g * group + at, ch)

    def chunk(g, h, row):
        return pl.ds(chunk_at(g, h, row), ch)

    def each(low_end, high_end, do):
        def step(i, carry):
            do(i)
            return carry

        lax.fori_loop(low_end, high_end, step, 0)

    def others(low_end, high_end, do):
        def step(i):
            @pl.when(jnp.logical_not(jnp.logical_and(is_mid, i == PLANE)))
            def _():
                do(i)

        each(low_end, high_end, step)

    barrier = pltpu.get_barrier_semaphore()

    def greet(row, col):
        pl.semaphore_signal(barrier, inc=1, device_id=(row, col), device_id_type=MESH)

    for d in range(1, NX):
        greet(across(d), c)
    greet(ry, c)
    greet(r, far_col)
    greet(r, up_col)
    greet(r, down_col)
    others(1, NROW, lambda i: greet(i, ahead(i)))

    @pl.when(r > 0)
    def _():
        others(0, NROW, lambda e: greet(e, source_col))

    def cov_copy(i):
        rows = pl.ds(i * tile, tile)
        return pltpu.make_async_copy(cov_ref.at[0, 0, rows], cov_f.at[rows], cov_sem.at[i])

    def cov_ready(i):
        cov_copy(i).wait()
        add_rows(cov, i * tile, tile, [(cov_f, i * tile)])

    slab_copy = pltpu.make_async_copy(far_ref.at[0], slab_f, slab_sem)
    slab_copy.start()
    for i in range(tiles):
        cov_copy(i).start()

    def partial_keys(g):
        for at in range(g * group, (g + 1) * group, 128):
            relative = edit_ref[:, at : at + 128] - r * tok_dev
            slots = lax.broadcasted_iota(jnp.int32, (tok_dev, 128), 0)
            total = jnp.zeros((tok_dev, 128), F32)
            for j in range(edit_ref.shape[0]):
                total = total + (relative[j : j + 1, :] == slots).astype(F32)
            counts[at : at + 128, :] = (total / edit_ref.shape[0]).T.astype(BF16)

        def step(n):
            columns = pl.ds(pl.multiple_of(n * tile, tile), tile)
            part[pl.ds(g * group, group), columns] = jnp.dot(
                counts[pl.ds(g * group, group), :], tok_ref[:, columns], preferred_element_type=F32
            ).astype(BF16)

        each(0, tiles, step)

    class Scatter:
        def __init__(self, src, ra1, ra2, rb1, rb2, sa, sb, ss, rs):
            self.src, self.ra1, self.ra2, self.rb1, self.rb2 = src, ra1, ra2, rb1, rb2
            self.sa, self.sb, self.ss, self.rs = sa, sb, ss, rs

        def a1(self, g, d):
            rows = pl.ds(pl.multiple_of(g * group + ((x + d) % NX) * (2 * ch), 2 * ch), 2 * ch)
            return remote(
                self.src.at[rows], self.ra1.at[g, d - 1], self.ss.at[g, d - 1], self.rs.at[g, d - 1], across(d), c
            )

        def b1(self, g):
            rows = pl.ds(pl.multiple_of(g * group + half + (1 - yl) * (NX * ch), NX * ch), NX * ch)
            return remote(self.src.at[rows], self.rb1.at[g], self.ss.at[g, 3], self.rs.at[g, 3], ry, c)

        def a2(self, g):
            rows = pl.ds(pl.multiple_of((1 - yl) * ch, ch), ch)
            return remote(self.sa.at[g, rows], self.ra2.at[g], self.ss.at[g, 4], self.rs.at[g, 4], ry, c)

        def b2(self, g, d):
            rows = pl.ds(pl.multiple_of(((x + d) % NX) * ch, ch), ch)
            return remote(
                self.sb.at[g, rows], self.rb2.at[g, d - 1], self.ss.at[g, 4 + d], self.rs.at[g, 4 + d], across(d), c
            )

        def start(self, g):
            for d in (1, 3, 2):
                self.a1(g, d).start()
            self.b1(g).start()

        def middle(self, g):
            self.b1(g).wait_recv()
            add_rows(
                self.sb.at[g], 0, NX * ch, [(self.src, g * group + half + yl * (NX * ch)), (self.rb1.at[g], 0)]
            )
            for d in (1, 3, 2):
                self.b2(g, d).start()
            for d in range(1, NX):
                self.a1(g, d).wait_recv()
            add_rows(
                self.sa.at[g], 0, 2 * ch,
                [(self.src, g * group + x * (2 * ch))] + [(self.ra1.at[g, d], 0) for d in range(NX - 1)],
            )
            self.a2(g).start()

        def end(self, g, out, a_more, b_more):
            self.a2(g).wait_recv()
            add_rows(out, chunk_at(g, 0, r), ch, [(self.sa.at[g], yl * ch), (self.ra2.at[g], 0)] + a_more)
            for d in range(1, NX):
                self.b2(g, d).wait_recv()
            add_rows(
                out, chunk_at(g, 1, r), ch,
                [(self.sb.at[g], x * ch)] + [(self.rb2.at[g, d], 0) for d in range(NX - 1)] + b_more,
            )

        def sent(self, g):
            self.b1(g).wait_send()
            self.a2(g).wait_send()
            for d in range(1, NX):
                self.a1(g, d).wait_send()
                self.b2(g, d).wait_send()

    class Gather:
        def __init__(self, full, ss, rs):
            self.full, self.ss, self.rs = full, ss, rs

        def move(self, g, rows, sem, row):
            return remote(
                self.full.at[rows], self.full.at[rows], self.ss.at[g, sem], self.rs.at[g, sem], row, c
            )

        def a1(self, g, row):
            return self.move(g, chunk(g, 0, row), 0, ry)

        def b1(self, g, row, d):
            return self.move(g, chunk(g, 1, row), d, across(d))

        def a2(self, g, xx, d):
            rows = pl.ds(pl.multiple_of(g * group + xx * (2 * ch), 2 * ch), 2 * ch)
            return self.move(g, rows, 3 + d, across(d))

        def b2(self, g, yy):
            rows = pl.ds(pl.multiple_of(g * group + half + yy * (NX * ch), NX * ch), NX * ch)
            return self.move(g, rows, 7, ry)

        def start(self, g):
            self.a1(g, r).start()
            for d in (1, 3, 2):
                self.b1(g, r, d).start()

        def middle(self, g):
            self.a1(g, ry).wait_recv()
            for d in (1, 3, 2):
                self.a2(g, x, d).start()
            for d in range(1, NX):
                self.b1(g, yl * NX + behind(d), d).wait_recv()
            self.b2(g, yl).start()

        def end(self, g):
            for d in range(1, NX):
                self.a2(g, behind(d), d).wait_recv()
            self.b2(g, 1 - yl).wait_recv()

        def sent(self, g):
            self.a1(g, r).wait_send()
            for d in range(1, NX):
                self.b1(g, r, d).wait_send()
                self.a2(g, x, d).wait_send()
            self.b2(g, yl).wait_send()

    def relay_copy(g, h, far):
        return remote(
            own.at[chunk(g, h, r)], relay.at[far, g, h], rel_s.at[far, g, h], rel_r.at[far, g, h], r,
            far_col if far else up_col,
        )

    def lag_copy(g, h, source, i, held):
        return remote(
            held, lag.at[chunk(g, h, source)], lag_s.at[i, g, h], lag_r.at[source, g, h], i, ahead(i)
        )

    def own_on(g, h):
        def send(i):
            lag_copy(g, h, r, i, own.at[chunk(g, h, r)]).start()

        return send

    def relay_on(g, h, far):
        def send(i):
            lag_copy(g, h, r, i, relay.at[far, g, h]).start()

        return send

    def lag_stay(g, h):
        return pltpu.make_async_copy(relay.at[0, g, h], lag.at[chunk(g, h, r)], stay_sem.at[0, g, h])

    def mir_copy(g, h, e, slot):
        return remote(
            mir.at[chunk(g, h, e)], m_in.at[slot, g, h], mir_s.at[e, g, h], mir_r.at[slot, g, h], e, source_col
        )

    def mir_stay(g, h):
        return pltpu.make_async_copy(mir.at[chunk(g, h, r)], m_in.at[PLANE - 1, g, h], stay_sem.at[1, g, h])

    def cross_copy(g, far):
        return remote(
            crossed.at[far, g], cross_in.at[far, g], cross_s.at[far, g], cross_r.at[far, g], r,
            far_col if far else down_col,
        )

    def add_slots(out, g, first, last):
        for h in range(2):
            for at in range(0, ch, SLAB):
                rows = pl.ds(at, SLAB)
                total = lax.fori_loop(
                    first, last,
                    lambda slot, so_far: so_far + m_in[slot, g, h, rows, :].astype(F32),
                    jnp.zeros((SLAB, width), F32),
                )
                out[pl.ds(h * ch + at, SLAB), :] = total.astype(out.dtype)

    at_0 = r * far_rows
    at_1 = width // 2 + r * far_rows
    start_0 = pl.multiple_of(at_0 // 128 * 128, 128)
    start_1 = pl.multiple_of(jnp.minimum(at_1 // 128 * 128, width - tile), 128)

    def rows_of(g):
        return pl.ds(g * group, group)

    def slab_far():
        return remote(slab_send, slab_in, slab_s, slab_r, r, far_col)

    def win_far(g, h):
        columns = pl.ds(start_0 if h == 0 else start_1, tile)
        return remote(
            own.at[rows_of(g), columns], win.at[rows_of(g), pl.ds(h * tile, tile)],
            win_s.at[g, h], win_r.at[g, h], r, far_col,
        )

    def nout_far(g):
        return remote(nout_send.at[rows_of(g)], nout.at[rows_of(g)], nout_s.at[g], nout_r.at[g], r, far_col)

    k_scatter = Scatter(part, k_ra1, k_ra2, k_rb1, k_rb2, k_sa, k_sb, krs_s, krs_r)
    q_scatter = Scatter(direct, q_ra1, q_ra2, q_rb1, q_rb2, q_sa, q_sb, qrs_s, qrs_r)
    k_gather = Gather(own, kag_s, kag_r)
    q_gather = Gather(q_all, qag_s, qag_r)
    contract_last = (((1,), (1,)), ((), ()))

    partial_keys(0)
    pl.semaphore_wait(barrier, 14 + jnp.where(r > 0, NROW, 0) - jnp.where(is_mid, 2, 0))
    k_scatter.start(0)
    for g in range(1, GROUPS):
        partial_keys(g)
        k_scatter.start(g)

    slab_copy.wait()

    @pl.when(low)
    def _():
        add_rows(slab_send, 0, far_rows, [(slab_f, 0)])
        slab_far().start()

    for i in range(2):
        cov_ready(i)
    for g in groups:
        k_scatter.middle(g)
    for i in range(2, 4):
        cov_ready(i)

    for g in groups:
        k_scatter.end(g, own, [], [])
        k_gather.start(g)
        for h in range(2):
            relay_copy(g, h, 0).start()

        @pl.when(u > 0)
        def _(g=g):
            for h in range(2):
                relay_copy(g, h, 1).start()

    for g in groups:
        k_gather.middle(g)
        for h in range(2):
            each(1, PLANE - u, own_on(g, h))

    for g in groups:
        for h in range(2):
            relay_copy(g, h, 0).wait_recv()
            others(PLANE - u, 2 * PLANE - u, relay_on(g, h, 0))

        @pl.when(is_mid)
        def _(g=g):
            for h in range(2):
                lag_stay(g, h).start()

        @pl.when(u > 0)
        def _(g=g):
            for h in range(2):
                relay_copy(g, h, 1).wait_recv()
                each(2 * PLANE - u, NROW, relay_on(g, h, 1))

    for i in range(4, tiles):
        cov_ready(i)

    @pl.when(jnp.logical_not(low))
    def _():
        slab_pad[...] = jnp.zeros_like(slab_pad)
        add_rows(slab_pad, tile + at_1 - start_1, far_rows, [(slab_f, 0)])
        slab_far().wait_recv()
        add_rows(slab_pad, at_0 - start_0, far_rows, [(slab_in, 0)])

    for g in groups:
        k_gather.end(g)

        @pl.when(low)
        def _(g=g):
            for h in range(2):
                win_far(g, h).start()

        @pl.when(r > 0)
        def _(g=g):
            def mirror(n):
                block = pl.ds(pl.multiple_of(n * tile, tile), tile)
                mir[rows_of(g), block] = lax.dot_general(
                    own[rows_of(g), :], cov[block, :], contract_last, preferred_element_type=F32
                ).astype(BF16)

            each(0, tiles, mirror)

            for h in range(2):
                others(0, NROW, lambda e, h=h: mir_copy(g, h, e, r - 1).start())

        @pl.when(is_mid)
        def _(g=g):
            for h in range(2):
                mir_stay(g, h).start()

        @pl.when(jnp.logical_not(low))
        def _(g=g):
            def narrow(n):
                block = pl.ds(pl.multiple_of(n * tile, tile), tile)
                nout_send[rows_of(g), block] = lax.dot_general(
                    own[rows_of(g), :], slab_pad[block, :], contract_last, preferred_element_type=F32
                ).astype(BF16)

            each(0, 2, narrow)
            nout_far(g).start()

    for g in groups:
        own_to_lag = pltpu.make_async_copy(own.at[rows_of(g)], lag.at[rows_of(g)], loc_sem)

        @pl.when(r == 0)
        def _(own_to_lag=own_to_lag):
            own_to_lag.start()
            own_to_lag.wait()

        @pl.when(r > 0)
        def _(g=g):
            def got_lag(e):
                for h in range(2):
                    lag_copy(g, h, e, 1, own.at[chunk(g, h, r)]).wait_recv()

            others(0, NROW, got_lag)

        @pl.when(is_mid)
        def _(g=g):
            for h in range(2):
                lag_stay(g, h).wait()

        @pl.when(low)
        def _(g=g):
            def step(n):
                block = pl.ds(pl.multiple_of(n * tile, tile), tile)
                direct[rows_of(g), block] = jnp.dot(
                    lag[rows_of(g), :], cov[:, block], preferred_element_type=F32
                ).astype(BF16)

            each(0, tiles, step)
            nout_far(g).wait_recv()

            def add_narrow(i):
                rows = pl.ds(pl.multiple_of(g * group + i * 64, 64), 64)
                for h, start in ((0, start_0), (1, start_1)):
                    columns = pl.ds(start, tile)
                    direct[rows, columns] = (
                        direct[rows, columns].astype(F32)
                        + nout[rows, pl.ds(h * tile, tile)].astype(F32)
                    ).astype(BF16)

            each(0, group // 64, add_narrow)

        @pl.when(jnp.logical_not(low))
        def _(g=g):
            for h in range(2):
                win_far(g, h).wait_recv()

            def step(n):
                block = pl.ds(pl.multiple_of(n * tile, tile), tile)
                direct[rows_of(g), block] = (
                    jnp.dot(lag[rows_of(g), :], cov[:, block], preferred_element_type=F32)
                    + jnp.dot(win[rows_of(g), :], slab_pad[:, block], preferred_element_type=F32)
                ).astype(BF16)

            each(0, tiles, step)

        q_scatter.start(g)

    for g in groups:
        def got_mir(i, g=g):
            for h in range(2):
                mir_copy(g, h, r, i - 1).wait_recv()

        others(1, NROW, got_mir)

        @pl.when(is_mid)
        def _(g=g):
            for h in range(2):
                mir_stay(g, h).wait()

        add_slots(crossed.at[0, g], g, PLANE - u - 1, 2 * PLANE - u - 1)
        cross_copy(g, 0).start()

        @pl.when(u > 0)
        def _(g=g):
            add_slots(crossed.at[1, g], g, 2 * PLANE - u - 1, NROW - 1)
            cross_copy(g, 1).start()

        add_slots(q_sum.at[g], g, 0, PLANE - u - 1)
        q_scatter.middle(g)

    for g in groups:
        cross_copy(g, 0).wait_recv()
        total = q_sum.at[g]
        add_rows(total, 0, 2 * ch, [(total, 0), (cross_in.at[0, g], 0)])

        @pl.when(u > 0)
        def _(g=g, total=total):
            cross_copy(g, 1).wait_recv()
            add_rows(total, 0, 2 * ch, [(total, 0), (cross_in.at[1, g], 0)])

        q_scatter.end(g, q_all, [(total, 0)], [(total, ch)])
        q_gather.start(g)

    def result(g):
        return pltpu.make_async_copy(q_all.at[rows_of(g)], out_ref.at[rows_of(g)], out_sem.at[g])

    for g in groups:
        q_gather.middle(g)
    for g in groups:
        q_gather.end(g)
        result(g).start()

    for g in groups:
        k_scatter.sent(g)
        q_scatter.sent(g)
        k_gather.sent(g)
        q_gather.sent(g)

        def lag_sent(i, g=g):
            for h in range(2):
                lag_copy(g, h, r, i, own.at[chunk(g, h, r)]).wait_send()

        others(1, NROW, lag_sent)

        @pl.when(r > 0)
        def _(g=g):
            def mir_sent(e):
                for h in range(2):
                    mir_copy(g, h, e, r - 1).wait_send()

            others(0, NROW, mir_sent)

        for h in range(2):
            relay_copy(g, h, 0).wait_send()
        cross_copy(g, 0).wait_send()

        @pl.when(u > 0)
        def _(g=g):
            for h in range(2):
                relay_copy(g, h, 1).wait_send()
            cross_copy(g, 1).wait_send()

        @pl.when(low)
        def _(g=g):
            for h in range(2):
                win_far(g, h).wait_send()

        @pl.when(jnp.logical_not(low))
        def _(g=g):
            nout_far(g).wait_send()

    @pl.when(low)
    def _():
        slab_far().wait_send()

    for g in groups:
        result(g).wait()


def delta_kernel(residual_ref, q_ref, out_ref):
    out_ref[...] = jnp.dot(residual_ref[...], q_ref[...], preferred_element_type=F32).astype(
        out_ref.dtype
    )


def shards(tokens, edit_src, cov_tiles, cov_far, residual):
    edits, context = edit_src.shape
    tok_dev, width = tokens.shape
    ch = edits // GROUPS // 2 // NROW
    far_rows = cov_far.shape[1]
    tiles = width // 256

    def buf(*shape, dtype=BF16):
        return pltpu.VMEM(shape, dtype)

    def dma(*shape):
        return pltpu.SemaphoreType.DMA(shape)

    def reduce_bufs():
        return [
            buf(GROUPS, NX - 1, 2 * ch, width), buf(GROUPS, ch, width), buf(GROUPS, NX * ch, width),
            buf(GROUPS, NX - 1, ch, width), buf(GROUPS, 2 * ch, width), buf(GROUPS, NX * ch, width),
        ]

    q_block = pl.pallas_call(
        kernel,
        name="edit_product",
        out_shape=jax.ShapeDtypeStruct((edits, width), BF16),
        in_specs=[
            pl.BlockSpec(memory_space=pltpu.VMEM),
            pl.BlockSpec(memory_space=pltpu.VMEM),
            pl.BlockSpec(memory_space=pl.ANY),
            pl.BlockSpec(memory_space=pl.ANY),
        ],
        out_specs=pl.BlockSpec(memory_space=pl.ANY),
        scratch_shapes=[
            buf(edits, tok_dev), buf(edits, width),
            buf(width, width, dtype=F32), buf(width, width),
            buf(far_rows, width, dtype=F32), buf(far_rows, width), buf(far_rows, width), buf(512, width),
            buf(edits, width), buf(edits, width), buf(edits, width), buf(edits, width),
            buf(edits, 512), buf(edits, 512), buf(edits, 512),
            *reduce_bufs(),
            *reduce_bufs(),
            buf(NROW - 1, GROUPS, 2, ch, width), buf(GROUPS, 2 * ch, width, dtype=F32), buf(edits, width),
            buf(2, GROUPS, 2, ch, width), buf(2, GROUPS, 2 * ch, width), buf(2, GROUPS, 2 * ch, width),
            dma(tiles), pltpu.SemaphoreType.DMA, pltpu.SemaphoreType.DMA, dma(GROUPS),
            *[dma(GROUPS, 8) for _ in range(8)],
            dma(NROW, GROUPS, 2), dma(NROW, GROUPS, 2), dma(NROW, GROUPS, 2), dma(NROW - 1, GROUPS, 2),
            pltpu.SemaphoreType.DMA, pltpu.SemaphoreType.DMA,
            dma(GROUPS, 2), dma(GROUPS, 2), dma(GROUPS), dma(GROUPS),
            dma(2, GROUPS, 2), dma(2, GROUPS, 2), dma(2, GROUPS), dma(2, GROUPS), dma(2, GROUPS, 2),
        ],
        compiler_params=pltpu.CompilerParams(
            collective_id=0, has_side_effects=True, vmem_limit_bytes=60 * 2**20
        ),
    )(edit_src.T, tokens, cov_tiles, cov_far)

    rows = residual.shape[0]
    step = 256
    return pl.pallas_call(
        delta_kernel,
        name="delta",
        grid=(rows // step,),
        out_shape=jax.ShapeDtypeStruct((rows, width), BF16),
        in_specs=[
            pl.BlockSpec((step, edits), lambda i: (i, 0)),
            pl.BlockSpec((edits, width), lambda i: (0, 0)),
        ],
        out_specs=pl.BlockSpec((step, width), lambda i: (i, 0)),
        compiler_params=pltpu.CompilerParams(vmem_limit_bytes=32 * 2**20),
    )(residual, q_block)


def solution(mesh):
    placed = (
        P("row", "col"),
        P(),
        P("row", "col", None, None),
        P("col", "row", None),
        P("row", None),
    )
    return jax.shard_map(
        shards, mesh=mesh, in_specs=placed, out_specs=P("row", "col"), check_vma=False
    )
```

time: 416 us -> 137 us (0.33)
  the two profiles are of different devices: /device:TPU:0 before, /device:TPU:34 now
where the time goes in v3:
time: 137 us
  Pallas kernels  136 us (99%)
  local copies, waits for them, and re-layouts  1.5 us (1%)
    pallas_call x1, Pallas kernels, shards(): pl.pallas_call(kernel, name='edit_product', out_shape=jax.ShapeDtypeStruc...  132 us
    pallas_call x1, Pallas kernels, shards(): pl.pallas_call(delta_kernel, name='delta', grid=(rows // step,), out_shap...  3.79 us

profile of v3, /device:TPU:34, one launch (start us, length us, event | category | flops | bytes accessed | tf_op | source)
XLA Modules:
  0.0 137.2 jit_solution(3613507325234101359)
XLA Ops:
  0.0 0.0 copy-start.1
  0.0 131.9 %edit_product.1.q_ref = bf16[512,1792]{1,0:T(8,128)(2,1)} custom-call(s32[4,512]{1,0:T(4,128)} %bitcast.1, bf16[256,1792]{1,0:T(8,128)(2,1)} %tok_ref.1, f32[1,1,1792,1792]{3,2,1,0:T(8,128)} %cov_ref.1, f32[1,112,1792]{2,1,0:T(8,128)} %far_ref.1), custom_call_target="tpu_custom_call" | custom-call | tf_op jit(solution)/shard_map/edit_product/pallas_call | solution.py:626
  131.9 0.0 copy-done.1
  131.9 0.0 copy-start
  131.9 1.5 %copy-done = bf16[512,1792]{1,0:T(8,128)(2,1)S(1)} copy-done((bf16[512,1792]{1,0:T(8,128)(2,1)S(1)}, bf16[512,1792]{1,0:T(8,128)(2,1)}, u32[]{:S(2)}) %copy-start) | copy-done | bytes 1835032
  133.4 3.8 %delta.1 = bf16[1024,1792]{1,0:T(8,128)(2,1)} custom-call(bf16[1024,512]{1,0:T(8,128)(2,1)S(1)} %copy-done.1, bf16[512,1792]{1,0:T(8,128)(2,1)S(1)} %copy-done), custom_call_target="tpu_custom_call" | custom-call | tf_op jit(solution)/shard_map/delta/pallas_call | solution.py:661
Async XLA Ops:
  0.0 131.9 %copy-start.1 = (bf16[1024,512]{1,0:T(8,128)(2,1)S(1)}, bf16[1024,512]{1,0:T(8,128)(2,1)}, u32[]{:S(2)}) copy-start(bf16[1024,512]{1,0:T(8,128)(2,1)} %residual_ref.1) | copy-start | bytes 3145732
  131.9 1.5 %copy-start = (bf16[512,1792]{1,0:T(8,128)(2,1)S(1)}, bf16[512,1792]{1,0:T(8,128)(2,1)}, u32[]{:S(2)}) copy-start(bf16[512,1792]{1,0:T(8,128)(2,1)} %edit_product.1.q_ref) | copy-start | bytes 5505028

commit v4 on v3

--- a/solution.py
+++ b/solution.py
@@ -47,11 +47,11 @@
     counts, part, cov_f, cov, slab_f, slab_send, slab_in, slab_pad,
     own, lag, mir, direct, win, nout_send, nout,
     k_ra1, k_ra2, k_rb1, k_rb2, k_sa, k_sb,
-    q_ra1, q_ra2, q_rb1, q_rb2, q_sa, q_sb, m_in, q_sum, q_all, relay, crossed, cross_in,
+    q_ra1, q_ra2, q_rb1, q_rb2, q_sa, q_sb, m_in, q_sum, q_all, held, mid, crossed, cross_in,
     cov_sem, slab_sem, loc_sem, out_sem,
     krs_s, krs_r, kag_s, kag_r, qrs_s, qrs_r, qag_s, qag_r,
-    lag_s, lag_r, mir_s, mir_r, slab_s, slab_r, win_s, win_r, nout_s, nout_r,
-    rel_s, rel_r, cross_s, cross_r, stay_sem,
+    first_s, first_r, second_s, second_r, mir_s, mir_r, slab_s, slab_r, win_s, win_r, nout_s, nout_r,
+    rel_s, rel_r, cross_s, cross_r, stay_sem, keep_sem,
 ):
     r = lax.axis_index("row")
     c = lax.axis_index("col")
@@ -124,10 +124,16 @@
     greet(r, up_col)
     greet(r, down_col)
     others(1, NROW, lambda i: greet(i, ahead(i)))
-
-    @pl.when(r > 0)
-    def _():
-        others(0, NROW, lambda e: greet(e, source_col))
+    for d in range(NX):
+        lag_by = yl * NX + (x + d) % NX
+
+        @pl.when(lag_by > 0)
+        def _(lag_by=lag_by):
+            greet(x, plane + (u + NROW - lag_by) % PLANE)
+
+            @pl.when(lag_by != PLANE)
+            def _():
+                greet(NX + x, plane + (u + NROW - lag_by) % PLANE)
 
     def cov_copy(i):
         rows = pl.ds(i * tile, tile)
@@ -271,29 +277,110 @@
 
     def relay_copy(g, h, far):
         return remote(
-            own.at[chunk(g, h, r)], relay.at[far, g, h], rel_s.at[far, g, h], rel_r.at[far, g, h], r,
+            held.at[0, g, h], held.at[1 + far, g, h], rel_s.at[far, g, h], rel_r.at[far, g, h], r,
             far_col if far else up_col,
         )
 
-    def lag_copy(g, h, source, i, held):
+    def lag_first(g, h, by, source, from_y):
+        y, d = by // NX, (by % NX + NX - x) % NX
+        place = mid.at[d, g, h, pl.ds(pl.multiple_of(from_y * ch, ch), ch)]
         return remote(
-            held, lag.at[chunk(g, h, source)], lag_s.at[i, g, h], lag_r.at[source, g, h], i, ahead(i)
+            source, place, first_s.at[by, g, h], first_r.at[d, from_y, g, h], y * NX + x, ahead(by)
         )
 
-    def own_on(g, h):
-        def send(i):
-            lag_copy(g, h, r, i, own.at[chunk(g, h, r)]).start()
-
-        return send
-
-    def relay_on(g, h, far):
-        def send(i):
-            lag_copy(g, h, r, i, relay.at[far, g, h]).start()
-
-        return send
-
     def lag_stay(g, h):
-        return pltpu.make_async_copy(relay.at[0, g, h], lag.at[chunk(g, h, r)], stay_sem.at[0, g, h])
+        return pltpu.make_async_copy(
+            held.at[1, g, h], mid.at[(NX - x) % NX, g, h, pl.ds(ch, ch)], keep_sem.at[g, h]
+        )
+
+    def here(by):
+        return jnp.logical_and(yl == 1, by == PLANE)
+
+    def lag_send(g, level, first, last):
+        def send(by):
+            @pl.when(jnp.logical_not(here(by)))
+            def _():
+                for h in range(2):
+                    lag_first(g, h, by, held.at[level, g, h], yl).start()
+
+        each(first, last, send)
+
+    def lag_relayed(g):
+        for h in range(2):
+            relay_copy(g, h, 0).wait_recv()
+        lag_send(g, 1, PLANE - u, 2 * PLANE - u)
+
+        @pl.when(yl == 1)
+        def _():
+            for h in range(2):
+                lag_stay(g, h).start()
+
+        @pl.when(u > 0)
+        def _():
+            for h in range(2):
+                relay_copy(g, h, 1).wait_recv()
+            lag_send(g, 2, 2 * PLANE - u, NROW)
+
+    def lag_got(g, h, d):
+        by = across(d)
+        lag_first(g, h, by, held.at[0, g, h], 0).wait_recv()
+
+        @pl.when(here(by))
+        def _():
+            lag_stay(g, h).wait()
+
+        @pl.when(jnp.logical_not(here(by)))
+        def _():
+            lag_first(g, h, by, held.at[0, g, h], 1).wait_recv()
+
+    def lag_second(g, d, part_at, xx):
+        if part_at == 0:
+            source = mid.at[d, g, 0]
+            rows = pl.ds(pl.multiple_of(g * group + xx * (2 * ch), 2 * ch), 2 * ch)
+        else:
+            source = mid.at[d, g, 1, pl.ds((part_at - 1) * ch, ch)]
+            rows = chunk(g, 1, (part_at - 1) * NX + xx)
+        return remote(
+            source, lag.at[rows], second_s.at[d - 1, g, part_at], second_r.at[d - 1, g, part_at], across(d), c
+        )
+
+    def passing(d, do):
+        @pl.when(across(d) > 0)
+        def _():
+            do(d)
+
+    def lag_pass(g):
+        def on(d):
+            for h in range(2):
+                lag_got(g, h, d)
+                for part_at in (0,) if h == 0 else (1, 2):
+                    lag_second(g, d, part_at, x).start()
+
+        for d in (1, 3, 2):
+            passing(d, on)
+
+    def lag_sent(g):
+        def first_sent(by):
+            @pl.when(jnp.logical_not(here(by)))
+            def _():
+                for h in range(2):
+                    lag_first(g, h, by, held.at[0, g, h], yl).wait_send()
+
+        each(1, NROW, first_sent)
+        for h in range(2):
+            relay_copy(g, h, 0).wait_send()
+
+        @pl.when(u > 0)
+        def _():
+            for h in range(2):
+                relay_copy(g, h, 1).wait_send()
+
+        def on(d):
+            for part_at in range(3):
+                lag_second(g, d, part_at, x).wait_send()
+
+        for d in range(1, NX):
+            passing(d, on)
 
     def mir_copy(g, h, e, slot):
         return remote(
@@ -301,7 +388,7 @@
         )
 
     def mir_stay(g, h):
-        return pltpu.make_async_copy(mir.at[chunk(g, h, r)], m_in.at[PLANE - 1, g, h], stay_sem.at[1, g, h])
+        return pltpu.make_async_copy(mir.at[chunk(g, h, r)], m_in.at[PLANE - 1, g, h], stay_sem.at[g, h])
 
     def cross_copy(g, far):
         return remote(
@@ -348,7 +435,7 @@
     contract_last = (((1,), (1,)), ((), ()))
 
     partial_keys(0)
-    pl.semaphore_wait(barrier, 14 + jnp.where(r > 0, NROW, 0) - jnp.where(is_mid, 2, 0))
+    pl.semaphore_wait(barrier, 14 - yl + jnp.where(r > 0, NROW, 0) - jnp.where(is_mid, 1, 0))
     k_scatter.start(0)
     for g in range(1, GROUPS):
         partial_keys(g)
@@ -370,35 +457,24 @@
 
     for g in groups:
         k_scatter.end(g, own, [], [])
+        for h in range(2):
+            add_rows(held.at[0, g, h], 0, ch, [(own, chunk_at(g, h, r))])
+            relay_copy(g, h, 0).start()
+
+        @pl.when(u > 0)
+        def _(g=g):
+            for h in range(2):
+                relay_copy(g, h, 1).start()
+
         k_gather.start(g)
-        for h in range(2):
-            relay_copy(g, h, 0).start()
-
-        @pl.when(u > 0)
-        def _(g=g):
-            for h in range(2):
-                relay_copy(g, h, 1).start()
-
+        lag_send(g, 0, 1, PLANE - u)
+
+    for g in groups:
+        lag_relayed(g)
     for g in groups:
         k_gather.middle(g)
-        for h in range(2):
-            each(1, PLANE - u, own_on(g, h))
-
-    for g in groups:
-        for h in range(2):
-            relay_copy(g, h, 0).wait_recv()
-            others(PLANE - u, 2 * PLANE - u, relay_on(g, h, 0))
-
-        @pl.when(is_mid)
-        def _(g=g):
-            for h in range(2):
-                lag_stay(g, h).start()
-
-        @pl.when(u > 0)
-        def _(g=g):
-            for h in range(2):
-                relay_copy(g, h, 1).wait_recv()
-                each(2 * PLANE - u, NROW, relay_on(g, h, 1))
+    for g in groups:
+        lag_pass(g)
 
     for i in range(4, tiles):
         cov_ready(i)
@@ -457,16 +533,14 @@
 
         @pl.when(r > 0)
         def _(g=g):
-            def got_lag(e):
-                for h in range(2):
-                    lag_copy(g, h, e, 1, own.at[chunk(g, h, r)]).wait_recv()
-
-            others(0, NROW, got_lag)
-
-        @pl.when(is_mid)
-        def _(g=g):
-            for h in range(2):
-                lag_stay(g, h).wait()
+            for h in range(2):
+                lag_got(g, h, 0)
+            add_rows(lag, pl.multiple_of(g * group + x * (2 * ch), 2 * ch), 2 * ch, [(mid.at[0, g, 0], 0)])
+            for y in range(2):
+                add_rows(lag, chunk_at(g, 1, y * NX + x), ch, [(mid.at[0, g, 1], y * ch)])
+            for d in range(1, NX):
+                for part_at in range(3):
+                    lag_second(g, d, part_at, behind(d)).wait_recv()
 
         @pl.when(low)
         def _(g=g):
@@ -527,6 +601,7 @@
             cross_copy(g, 1).start()
 
         add_slots(q_sum.at[g], g, 0, PLANE - u - 1)
+    for g in groups:
         q_scatter.middle(g)
 
     for g in groups:
@@ -557,11 +632,7 @@
         k_gather.sent(g)
         q_gather.sent(g)
 
-        def lag_sent(i, g=g):
-            for h in range(2):
-                lag_copy(g, h, r, i, own.at[chunk(g, h, r)]).wait_send()
-
-        others(1, NROW, lag_sent)
+        lag_sent(g)
 
         @pl.when(r > 0)
         def _(g=g):
@@ -571,14 +642,10 @@
 
             others(0, NROW, mir_sent)
 
-        for h in range(2):
-            relay_copy(g, h, 0).wait_send()
         cross_copy(g, 0).wait_send()
 
         @pl.when(u > 0)
         def _(g=g):
-            for h in range(2):
-                relay_copy(g, h, 1).wait_send()
             cross_copy(g, 1).wait_send()
 
         @pl.when(low)
@@ -643,13 +710,14 @@
             *reduce_bufs(),
             *reduce_bufs(),
             buf(NROW - 1, GROUPS, 2, ch, width), buf(GROUPS, 2 * ch, width, dtype=F32), buf(edits, width),
-            buf(2, GROUPS, 2, ch, width), buf(2, GROUPS, 2 * ch, width), buf(2, GROUPS, 2 * ch, width),
+            buf(3, GROUPS, 2, ch, width), buf(NX, GROUPS, 2, 2 * ch, width), buf(2, GROUPS, 2 * ch, width), buf(2, GROUPS, 2 * ch, width),
             dma(tiles), pltpu.SemaphoreType.DMA, pltpu.SemaphoreType.DMA, dma(GROUPS),
             *[dma(GROUPS, 8) for _ in range(8)],
-            dma(NROW, GROUPS, 2), dma(NROW, GROUPS, 2), dma(NROW, GROUPS, 2), dma(NROW - 1, GROUPS, 2),
+            dma(NROW, GROUPS, 2), dma(NX, 2, GROUPS, 2), dma(NX - 1, GROUPS, 3), dma(NX - 1, GROUPS, 3),
+            dma(NROW, GROUPS, 2), dma(NROW - 1, GROUPS, 2),
             pltpu.SemaphoreType.DMA, pltpu.SemaphoreType.DMA,
             dma(GROUPS, 2), dma(GROUPS, 2), dma(GROUPS), dma(GROUPS),
-            dma(2, GROUPS, 2), dma(2, GROUPS, 2), dma(2, GROUPS), dma(2, GROUPS), dma(2, GROUPS, 2),
+            dma(2, GROUPS, 2), dma(2, GROUPS, 2), dma(2, GROUPS), dma(2, GROUPS), dma(GROUPS, 2), dma(GROUPS, 2),
         ],
         compiler_params=pltpu.CompilerParams(
             collective_id=0, has_side_effects=True, vmem_limit_bytes=60 * 2**20

time: 137 us -> 125 us (0.912)
  the two profiles are of different devices: /device:TPU:34 before, /device:TPU:0 now
where the time goes in v4:
time: 125 us; the launch traced here: 124 us
  Pallas kernels  122 us (98%)
  local copies, waits for them, and re-layouts  1.5 us (1%)
    pallas_call x1, Pallas kernels, shards(): pl.pallas_call(kernel, name='edit_product', out_shape=jax.ShapeDtypeStruc...  118 us
    pallas_call x1, Pallas kernels, shards(): pl.pallas_call(delta_kernel, name='delta', grid=(rows // step,), out_shap...  3.79 us

profile of v4, /device:TPU:0, one launch (start us, length us, event | category | flops | bytes accessed | tf_op | source)
XLA Modules:
  0.0 123.6 jit_solution(2705769763787973287)
XLA Ops:
  0.0 0.0 copy-start.1
  0.0 118.3 %edit_product.1.q_ref = bf16[512,1792]{1,0:T(8,128)(2,1)} custom-call(s32[4,512]{1,0:T(4,128)} %bitcast.1, bf16[256,1792]{1,0:T(8,128)(2,1)} %tok_ref.1, f32[1,1,1792,1792]{3,2,1,0:T(8,128)} %cov_ref.1, f32[1,112,1792]{2,1,0:T(8,128)} %far_ref.1), custom_call_target="tpu_custom_call" | custom-call | tf_op jit(solution)/shard_map/edit_product/pallas_call | solution.py:693
  118.3 0.0 copy-done.1
  118.3 0.0 copy-start
  118.3 1.5 %copy-done = bf16[512,1792]{1,0:T(8,128)(2,1)S(1)} copy-done((bf16[512,1792]{1,0:T(8,128)(2,1)S(1)}, bf16[512,1792]{1,0:T(8,128)(2,1)}, u32[]{:S(2)}) %copy-start) | copy-done | bytes 1835032
  119.8 3.8 %delta.1 = bf16[1024,1792]{1,0:T(8,128)(2,1)} custom-call(bf16[1024,512]{1,0:T(8,128)(2,1)S(1)} %copy-done.1, bf16[512,1792]{1,0:T(8,128)(2,1)S(1)} %copy-done), custom_call_target="tpu_custom_call" | custom-call | tf_op jit(solution)/shard_map/delta/pallas_call | solution.py:729
Async XLA Ops:
  0.0 118.3 %copy-start.1 = (bf16[1024,512]{1,0:T(8,128)(2,1)S(1)}, bf16[1024,512]{1,0:T(8,128)(2,1)}, u32[]{:S(2)}) copy-start(bf16[1024,512]{1,0:T(8,128)(2,1)} %residual_ref.1) | copy-start | bytes 3145732
  118.3 1.5 %copy-start = (bf16[512,1792]{1,0:T(8,128)(2,1)S(1)}, bf16[512,1792]{1,0:T(8,128)(2,1)}, u32[]{:S(2)}) copy-start(bf16[512,1792]{1,0:T(8,128)(2,1)} %edit_product.1.q_ref) | copy-start | bytes 5505028

commit v5 on v4

--- a/solution.py
+++ b/solution.py
@@ -46,8 +46,8 @@
     edit_ref, tok_ref, cov_ref, far_ref, out_ref,
     counts, part, cov_f, cov, slab_f, slab_send, slab_in, slab_pad,
     own, lag, mir, direct, win, nout_send, nout,
-    k_ra1, k_ra2, k_rb1, k_rb2, k_sa, k_sb,
-    q_ra1, q_ra2, q_rb1, q_rb2, q_sa, q_sb, m_in, q_sum, q_all, held, mid, crossed, cross_in,
+    k_ra1, k_ra2, k_rb1, k_rb2, k_sa, k_sb, k_pass, k_sum,
+    q_ra1, q_ra2, q_rb1, q_rb2, q_sa, q_sb, q_pass, q_part, m_in, q_sum, q_all, held, mid, crossed, cross_in,
     cov_sem, slab_sem, loc_sem, out_sem,
     krs_s, krs_r, kag_s, kag_r, qrs_s, qrs_r, qag_s, qag_r,
     first_s, first_r, second_s, second_r, mir_s, mir_r, slab_s, slab_r, win_s, win_r, nout_s, nout_r,
@@ -166,19 +166,33 @@
         each(0, tiles, step)
 
     class Scatter:
-        def __init__(self, src, ra1, ra2, rb1, rb2, sa, sb, ss, rs):
+        def __init__(self, src, ra1, ra2, rb1, rb2, sa, sb, passed, summed, ss, rs):
             self.src, self.ra1, self.ra2, self.rb1, self.rb2 = src, ra1, ra2, rb1, rb2
-            self.sa, self.sb, self.ss, self.rs = sa, sb, ss, rs
-
-        def a1(self, g, d):
-            rows = pl.ds(pl.multiple_of(g * group + ((x + d) % NX) * (2 * ch), 2 * ch), 2 * ch)
+            self.sa, self.sb, self.passed, self.summed, self.ss, self.rs = sa, sb, passed, summed, ss, rs
+
+        def half_at(self, g, d, part_at):
+            return pl.multiple_of(g * group + ((x + d) % NX) * (2 * ch) + part_at * ch, ch)
+
+        def a1(self, g, way, whole):
+            d = 1 if way == 0 else 3
+            if whole:
+                src, dst = self.half_at(g, d, 1 - way), self.ra1.at[g, way, pl.ds((1 - way) * ch, ch)]
+            else:
+                src, dst = self.half_at(g, 2, way), self.passed.at[g, way]
+            sem = 2 * way + (1 if whole else 0)
             return remote(
-                self.src.at[rows], self.ra1.at[g, d - 1], self.ss.at[g, d - 1], self.rs.at[g, d - 1], across(d), c
+                self.src.at[pl.ds(src, ch)], dst, self.ss.at[g, sem], self.rs.at[g, sem], across(d), c
+            )
+
+        def a1_on(self, g, way):
+            return remote(
+                self.summed.at[g, way], self.ra1.at[g, way, pl.ds(way * ch, ch)],
+                self.ss.at[g, 8 + way], self.rs.at[g, 8 + way], across(1 if way == 0 else 3), c,
             )
 
         def b1(self, g):
             rows = pl.ds(pl.multiple_of(g * group + half + (1 - yl) * (NX * ch), NX * ch), NX * ch)
-            return remote(self.src.at[rows], self.rb1.at[g], self.ss.at[g, 3], self.rs.at[g, 3], ry, c)
+            return remote(self.src.at[rows], self.rb1.at[g], self.ss.at[g, 10], self.rs.at[g, 10], ry, c)
 
         def a2(self, g):
             rows = pl.ds(pl.multiple_of((1 - yl) * ch, ch), ch)
@@ -191,22 +205,31 @@
             )
 
         def start(self, g):
-            for d in (1, 3, 2):
-                self.a1(g, d).start()
             self.b1(g).start()
+            for whole in (False, True):
+                for way in range(2):
+                    self.a1(g, way, whole).start()
 
         def middle(self, g):
+            for way in range(2):
+                self.a1(g, way, False).wait_recv()
+                at = self.half_at(g, 1 if way == 0 else 3, way)
+                add_rows(self.summed.at[g, way], 0, ch, [(self.src, at), (self.passed.at[g, way], 0)])
+                self.a1_on(g, way).start()
             self.b1(g).wait_recv()
             add_rows(
                 self.sb.at[g], 0, NX * ch, [(self.src, g * group + half + yl * (NX * ch)), (self.rb1.at[g], 0)]
             )
             for d in (1, 3, 2):
                 self.b2(g, d).start()
-            for d in range(1, NX):
-                self.a1(g, d).wait_recv()
+
+        def turn(self, g):
+            for way in range(2):
+                self.a1(g, way, True).wait_recv()
+                self.a1_on(g, way).wait_recv()
             add_rows(
                 self.sa.at[g], 0, 2 * ch,
-                [(self.src, g * group + x * (2 * ch))] + [(self.ra1.at[g, d], 0) for d in range(NX - 1)],
+                [(self.src, g * group + x * (2 * ch))] + [(self.ra1.at[g, way], 0) for way in range(2)],
             )
             self.a2(g).start()
 
@@ -223,8 +246,11 @@
         def sent(self, g):
             self.b1(g).wait_send()
             self.a2(g).wait_send()
+            for way in range(2):
+                self.a1(g, way, False).wait_send()
+                self.a1(g, way, True).wait_send()
+                self.a1_on(g, way).wait_send()
             for d in range(1, NX):
-                self.a1(g, d).wait_send()
                 self.b2(g, d).wait_send()
 
     class Gather:
@@ -246,6 +272,15 @@
             rows = pl.ds(pl.multiple_of(g * group + xx * (2 * ch), 2 * ch), 2 * ch)
             return self.move(g, rows, 3 + d, across(d))
 
+        def a2_on(self, g, xx, way):
+            rows = pl.ds(pl.multiple_of(g * group + xx * (2 * ch) + way * ch, ch), ch)
+            return self.move(g, rows, 8 + way, across(1 if way == 0 else 3))
+
+        def turn(self, g):
+            for way, d in ((0, 1), (1, 3)):
+                self.a2(g, behind(d), d).wait_recv()
+                self.a2_on(g, behind(d), way).start()
+
         def b2(self, g, yy):
             rows = pl.ds(pl.multiple_of(g * group + half + yy * (NX * ch), NX * ch), NX * ch)
             return self.move(g, rows, 7, ry)
@@ -257,22 +292,24 @@
 
         def middle(self, g):
             self.a1(g, ry).wait_recv()
-            for d in (1, 3, 2):
+            for d in (1, 3):
                 self.a2(g, x, d).start()
             for d in range(1, NX):
                 self.b1(g, yl * NX + behind(d), d).wait_recv()
             self.b2(g, yl).start()
 
         def end(self, g):
-            for d in range(1, NX):
-                self.a2(g, behind(d), d).wait_recv()
+            for way in range(2):
+                self.a2_on(g, (x + 2) % NX, way).wait_recv()
             self.b2(g, 1 - yl).wait_recv()
 
         def sent(self, g):
             self.a1(g, r).wait_send()
             for d in range(1, NX):
                 self.b1(g, r, d).wait_send()
+            for way, d in ((0, 1), (1, 3)):
                 self.a2(g, x, d).wait_send()
+                self.a2_on(g, behind(d), way).wait_send()
             self.b2(g, yl).wait_send()
 
     def relay_copy(g, h, far):
@@ -428,8 +465,8 @@
     def nout_far(g):
         return remote(nout_send.at[rows_of(g)], nout.at[rows_of(g)], nout_s.at[g], nout_r.at[g], r, far_col)
 
-    k_scatter = Scatter(part, k_ra1, k_ra2, k_rb1, k_rb2, k_sa, k_sb, krs_s, krs_r)
-    q_scatter = Scatter(direct, q_ra1, q_ra2, q_rb1, q_rb2, q_sa, q_sb, qrs_s, qrs_r)
+    k_scatter = Scatter(part, k_ra1, k_ra2, k_rb1, k_rb2, k_sa, k_sb, k_pass, k_sum, krs_s, krs_r)
+    q_scatter = Scatter(direct, q_ra1, q_ra2, q_rb1, q_rb2, q_sa, q_sb, q_pass, q_part, qrs_s, qrs_r)
     k_gather = Gather(own, kag_s, kag_r)
     q_gather = Gather(q_all, qag_s, qag_r)
     contract_last = (((1,), (1,)), ((), ()))
@@ -452,6 +489,8 @@
         cov_ready(i)
     for g in groups:
         k_scatter.middle(g)
+    for g in groups:
+        k_scatter.turn(g)
     for i in range(2, 4):
         cov_ready(i)
 
@@ -473,6 +512,8 @@
         lag_relayed(g)
     for g in groups:
         k_gather.middle(g)
+    for g in groups:
+        k_gather.turn(g)
     for g in groups:
         lag_pass(g)
 
@@ -603,6 +644,8 @@
         add_slots(q_sum.at[g], g, 0, PLANE - u - 1)
     for g in groups:
         q_scatter.middle(g)
+    for g in groups:
+        q_scatter.turn(g)
 
     for g in groups:
         cross_copy(g, 0).wait_recv()
@@ -622,6 +665,8 @@
 
     for g in groups:
         q_gather.middle(g)
+    for g in groups:
+        q_gather.turn(g)
     for g in groups:
         q_gather.end(g)
         result(g).start()
@@ -686,8 +731,9 @@
 
     def reduce_bufs():
         return [
-            buf(GROUPS, NX - 1, 2 * ch, width), buf(GROUPS, ch, width), buf(GROUPS, NX * ch, width),
+            buf(GROUPS, 2, 2 * ch, width), buf(GROUPS, ch, width), buf(GROUPS, NX * ch, width),
             buf(GROUPS, NX - 1, ch, width), buf(GROUPS, 2 * ch, width), buf(GROUPS, NX * ch, width),
+            buf(GROUPS, 2, ch, width), buf(GROUPS, 2, ch, width),
         ]
 
     q_block = pl.pallas_call(
@@ -712,7 +758,7 @@
             buf(NROW - 1, GROUPS, 2, ch, width), buf(GROUPS, 2 * ch, width, dtype=F32), buf(edits, width),
             buf(3, GROUPS, 2, ch, width), buf(NX, GROUPS, 2, 2 * ch, width), buf(2, GROUPS, 2 * ch, width), buf(2, GROUPS, 2 * ch, width),
             dma(tiles), pltpu.SemaphoreType.DMA, pltpu.SemaphoreType.DMA, dma(GROUPS),
-            *[dma(GROUPS, 8) for _ in range(8)],
+            *[dma(GROUPS, 12) for _ in range(8)],
             dma(NROW, GROUPS, 2), dma(NX, 2, GROUPS, 2), dma(NX - 1, GROUPS, 3), dma(NX - 1, GROUPS, 3),
             dma(NROW, GROUPS, 2), dma(NROW - 1, GROUPS, 2),
             pltpu.SemaphoreType.DMA, pltpu.SemaphoreType.DMA,

time: 125 us -> 122 us (0.976)
  Pallas kernels: 122 us -> 120 us
    pallas_call x1, Pallas kernels: 118 us -> 116 us  [shards(): pl.pallas_call(kernel, name='edit_product', out_shape=jax.ShapeDtypeStruc...]
where the time goes in v5:
time: 122 us; the launch traced here: 121 us
  Pallas kernels  120 us (98%)
  local copies, waits for them, and re-layouts  1.5 us (1%)
    pallas_call x1, Pallas kernels, shards(): pl.pallas_call(kernel, name='edit_product', out_shape=jax.ShapeDtypeStruc...  116 us
    pallas_call x1, Pallas kernels, shards(): pl.pallas_call(delta_kernel, name='delta', grid=(rows // step,), out_shap...  3.79 us

profile of v5, /device:TPU:0, one launch (start us, length us, event | category | flops | bytes accessed | tf_op | source)
XLA Modules:
  0.0 121.2 jit_solution(17207324284944119942)
XLA Ops:
  0.0 0.0 copy-start.1
  0.0 115.8 %edit_product.1.q_ref = bf16[512,1792]{1,0:T(8,128)(2,1)} custom-call(s32[4,512]{1,0:T(4,128)} %bitcast.1, bf16[256,1792]{1,0:T(8,128)(2,1)} %tok_ref.1, f32[1,1,1792,1792]{3,2,1,0:T(8,128)} %cov_ref.1, f32[1,112,1792]{2,1,0:T(8,128)} %far_ref.1), custom_call_target="tpu_custom_call" | custom-call | tf_op jit(solution)/shard_map/edit_product/pallas_call | solution.py:739
  115.9 0.0 copy-done.1
  115.9 0.0 copy-start
  115.9 1.5 %copy-done = bf16[512,1792]{1,0:T(8,128)(2,1)S(1)} copy-done((bf16[512,1792]{1,0:T(8,128)(2,1)S(1)}, bf16[512,1792]{1,0:T(8,128)(2,1)}, u32[]{:S(2)}) %copy-start) | copy-done | bytes 1835032
  117.4 3.8 %delta.1 = bf16[1024,1792]{1,0:T(8,128)(2,1)} custom-call(bf16[1024,512]{1,0:T(8,128)(2,1)S(1)} %copy-done.1, bf16[512,1792]{1,0:T(8,128)(2,1)S(1)} %copy-done), custom_call_target="tpu_custom_call" | custom-call | tf_op jit(solution)/shard_map/delta/pallas_call | solution.py:775
Async XLA Ops:
  0.0 115.9 %copy-start.1 = (bf16[1024,512]{1,0:T(8,128)(2,1)S(1)}, bf16[1024,512]{1,0:T(8,128)(2,1)}, u32[]{:S(2)}) copy-start(bf16[1024,512]{1,0:T(8,128)(2,1)} %residual_ref.1) | copy-start | bytes 3145732
  115.9 1.5 %copy-start = (bf16[512,1792]{1,0:T(8,128)(2,1)S(1)}, bf16[512,1792]{1,0:T(8,128)(2,1)}, u32[]{:S(2)}) copy-start(bf16[512,1792]{1,0:T(8,128)(2,1)} %edit_product.1.q_ref) | copy-start | bytes 5505028
